TPU v7x, 32 devices: a whole 2x2x4 slice. The times are simulated.
32 devices in a mesh: group: 2 (over x), node: 8 (over z, y), local: 2 (over core).
Axes of the slice: x: 2, y: 2, z: 4, core: 2. Of those that a mesh axis runs over, the one named last changes fastest.
Arguments:
- tokens: bfloat16 [2048, 3584], P(('group', 'node', 'local')), parts along dimension 0, may hold values from -6 to 6
- routes: int32 [2048, 8], P(('group', 'node', 'local')), parts along dimension 0, may hold values from 0 to 15, all different within a row; in each aligned block of 64 rows (0 to 63, 64 to 127, ...) at most 40 rows name the same one
- gate_values: bfloat16 [2048, 8], P(('group', 'node', 'local')), parts along dimension 0, may hold values from 0.049804688 to 0.29882812
- gate_weight: bfloat16 [16, 3584, 1024], P(('node', 'local')), may hold values from -0.09375 to 0.09375
- up_weight: bfloat16 [16, 3584, 1024], P(('node', 'local')), may hold values from -0.09375 to 0.09375
- down_weight: bfloat16 [16, 1024, 3584], P(('node', 'local')), may hold values from -0.1875 to 0.1875
Outputs:
- mixed: bfloat16 [2048, 3584], P(('group', 'node', 'local')), parts along dimension 0
There are 2 independent parts, one for each index of `group`. A program takes and returns all parts, laid end to end along the dimension named above; an argument that names none is the same for every part. Nothing has to cross between parts.
Inputs may be any that keep to these rules, and one draw needn't show every extreme that they name: `routes`: A token's 8 expert copies are distinct; of the 64 tokens of one device at most 40 name one expert copy, a bound that some block reaches of them.
All inputs are finite; a program needn't handle non-finite values.
Results may differ from a plain program's by a relative error of at most 0.0058.
Values may be sent and summed in bfloat16 or wider, within the bound.
No kernel may reach another device: no remote copies, remote signals or barrier semaphores. Data moves between devices by JAX's collectives and lax.ppermute only.
A program may use at most 128 MiB of HBM per device.

v0:
```python
import jax
import jax.numpy as jnp
from jax import lax
from jax.sharding import PartitionSpec as P


def expert(inputs, w_gate, w_up, w_down):
    gate_part = jnp.dot(inputs, w_gate, preferred_element_type=jnp.float32)
    upper_part = jnp.dot(inputs, w_up, preferred_element_type=jnp.float32)
    hidden = (jax.nn.silu(gate_part) * upper_part).astype(jnp.bfloat16)
    return jnp.dot(hidden, w_down, preferred_element_type=jnp.float32).astype(jnp.bfloat16)


def placement_of(route_ids, slot_count, capacity):
    flat_ids = route_ids.reshape(-1)
    one_hot = (flat_ids[:, None] == jnp.arange(slot_count, dtype=jnp.int32)[None, :]).astype(
        jnp.int32
    )
    before = jnp.cumsum(one_hot, axis=0, dtype=jnp.int32) - one_hot
    position = jnp.sum(before * one_hot, axis=1, dtype=jnp.int32)
    return flat_ids * capacity + position


def shards(tokens, routes, gate_values, gate_weight, up_weight, down_weight):
    tok_count, model_width = tokens.shape
    top_count = routes.shape[1]
    node_count = lax.axis_size("node")
    local_count = lax.axis_size("local")
    ep_devices = node_count * local_count
    capacity = 5 * tok_count * top_count // (4 * ep_devices)
    target = placement_of(routes, ep_devices, capacity)
    copies = jnp.repeat(tokens, top_count, axis=0)
    outgoing = jnp.zeros((ep_devices * capacity, model_width), jnp.bfloat16).at[target].set(copies)
    w_gate = gate_weight[0]
    w_up = up_weight[0]
    w_down = down_weight[0]
    flat_blocks = outgoing.reshape(ep_devices, capacity, model_width)
    received = lax.all_to_all(
        flat_blocks, ("node", "local"), split_axis=0, concat_axis=0, tiled=True
    )
    flat_rows = received.reshape(-1, model_width)
    computed = expert(flat_rows, w_gate, w_up, w_down).reshape(received.shape)
    returned = lax.all_to_all(computed, ("node", "local"), split_axis=0, concat_axis=0, tiled=True)
    returned = returned.reshape(ep_devices * capacity, model_width)
    picked = returned[target].astype(jnp.float32).reshape(tok_count, top_count, model_width)
    mixed = jnp.sum(picked * gate_values.astype(jnp.float32)[:, :, None], axis=1)
    return mixed.astype(jnp.bfloat16)


def solution(mesh):
    return jax.shard_map(
        shards,
        mesh=mesh,
        in_specs=(
            P(("group", "node", "local"), None),
            P(("group", "node", "local"), None),
            P(("group", "node", "local"), None),
            P(("node", "local"), None, None),
            P(("node", "local"), None, None),
            P(("node", "local"), None, None),
        ),
        out_specs=P(("group", "node", "local"), None),
        check_vma=False,
    )
```

profile of v0, /device:TPU:13, one launch (start us, length us, event | category | flops | bytes accessed | tf_op | source)
XLA Modules:
  0.0 268.4 jit_solution(16651000559379313981)
XLA Ops:
  0.0 0.0 copy-start
  0.0 0.8 copy.9
  0.8 0.1 eq.29
  0.9 0.1 eq.25
  1.0 0.7 broadcast_multiply_fusion
  1.7 1.1 reduce-window.6
  2.9 0.2 slice_reduce_fusion
  3.1 0.1 copy.8
  3.2 0.1 mul.36
  3.3 0.1 fusion.21
  3.4 0.0 copy-done
  3.4 8.2 %scatter_custom_fusion = bf16[640,3584]{1,0:T(8,128)(2,1)} fusion(s32[512]{0:T(512)S(1)} %bitcast.52, bf16[]{:T(256)} %constant.6.clone.1, bf16[64,3584]{1,0:T(8,128)(2,1)S(1)} %copy-done), kind=kCustom, calls=%fused_computation.11 | custom fusion | bytes 5046274 | tf_op jit(solution)/shard_map/scatter | solution.py:33
  11.6 107.2 %all_to_all.10 = bf16[16,40,3584]{2,1,0:T(8,128)(2,1)S(1)} all-to-all(bf16[16,40,3584]{2,1,0:T(8,128)(2,1)} %bitcast.48), channel_id=1, replica_groups=mesh['group'=2,'node'=8,'local'=2] {'node','local'}, dimensions={0} | all-to-all | bytes 9175040 | tf_op jit(solution)/shard_map/all_to_all | solution.py:38
  118.8 0.0 copy-start.1
  118.8 2.0 copy-done.1
  120.9 7.1 %fusion.5 = f32[640,1024]{1,0:T(8,128)S(1)} fusion(bf16[640,3584]{1,0:T(8,128)(2,1)S(1)} %bitcast.50, bf16[1,3584,1024]{2,1,0:T(8,128)(2,1)} %param.9), kind=kOutput, calls=%fused_computation.8 | convolution fusion | flops 4697620480 | bytes 14548992 | tf_op jit(solution)/shard_map/dot_general | solution.py:8
  128.0 17.4 %fusion.7 = bf16[640,3584]{1,0:T(8,128)(2,1)} fusion(bf16[1,1024,3584]{2,1,0:T(8,128)(2,1)} %param.11, f32[640,1024]{1,0:T(8,128)S(1)} %fusion.5, bf16[640,3584]{1,0:T(8,128)(2,1)} %bitcast.51, bf16[1,3584,1024]{2,1,0:T(8,128)(2,1)} %param.10), kind=kOutput, calls=%fused_computation.10 | convolution fusion | flops 9401466880 | bytes 26476544 | tf_op jit(solution)/shard_map/dot_general | solution.py:11
  145.4 0.0 copy-start.2
  145.4 5.5 %all-to-all-start.1 = ((bf16[16,40,3584]{2,1,0:T(8,128)(2,1)}), bf16[16,40,3584]{2,1,0:T(8,128)(2,1)}, u32[]{:S(2)}, u32[]{:S(2)}) async-start(bf16[16,40,3584]{2,1,0:T(8,128)(2,1)} %bitcast.49), calls=%async_computation.1 | async-start | bytes 9175040 | tf_op jit(solution)/shard_map/all_to_all | solution.py:43
  150.9 0.0 copy-done.2
  150.9 0.1 copy.12
  151.0 100.8 %all-to-all-done.1 = bf16[16,40,3584]{2,1,0:T(8,128)(2,1)} async-done(((bf16[16,40,3584]{2,1,0:T(8,128)(2,1)}), bf16[16,40,3584]{2,1,0:T(8,128)(2,1)}, u32[]{:S(2)}, u32[]{:S(2)}) %all-to-all-start.1) | async-done | bytes 4587552 | tf_op jit(solution)/shard_map/all_to_all | solution.py:43
  251.8 10.8 %gather_fusion = bf16[512,3584]{1,0:T(8,128)(2,1)} fusion(bf16[640,3584]{1,0:T(8,128)(2,1)} %bitcast.10, s32[1024]{0:T(1024)S(1)} %pad_clamp_fusion), kind=kCustom, calls=%fused_computation | custom fusion | bytes 7342080 | tf_op jit(solution)/shard_map/gather | solution.py:45
  262.6 5.8 %fusion = bf16[64,3584]{1,0:T(8,128)(2,1)} fusion(bf16[512,3584]{1,0:T(8,128)(2,1)} %gather_fusion, f32[64,8]{1,0:T(8,128)S(1)} %copy.12), kind=kLoop, calls=%fused_computation.3 | loop fusion | flops 5275648 | bytes 4130816 | tf_op jit(solution)/shard_map/reduce_sum | solution.py:46
  (5 shorter events, 0.1 us)
Async XLA Ops:
  0.0 3.4 %copy-start = (bf16[64,3584]{1,0:T(8,128)(2,1)S(1)}, bf16[64,3584]{1,0:T(8,128)(2,1)}, u32[]{:S(2)}) copy-start(bf16[64,3584]{1,0:T(8,128)(2,1)} %param.6) | copy-start | bytes 1376260
  118.8 2.1 copy-start.1
  145.4 5.5 %copy-start.2 = (bf16[64,8]{0,1:T(8,128)(2,1)S(1)}, bf16[64,8]{0,1:T(8,128)(2,1)}, u32[]{:S(2)}) copy-start(bf16[64,8]{0,1:T(8,128)(2,1)} %param.8) | copy-start | bytes 3076
  145.4 106.4 %all-to-all-start.1 = ((bf16[16,40,3584]{2,1,0:T(8,128)(2,1)}), bf16[16,40,3584]{2,1,0:T(8,128)(2,1)}, u32[]{:S(2)}, u32[]{:S(2)}) async-start(bf16[16,40,3584]{2,1,0:T(8,128)(2,1)} %bitcast.49), calls=%async_computation.1 | async-start | bytes 9175040 | tf_op jit(solution)/shard_map/all_to_all | solution.py:43
where the time goes:
time: 269 us; the launch traced here: 268 us
  blocking collectives  107 us (40%)
  waiting for transfers between devices  101 us (38%)
  matrix products  24.6 us (9%)
  local copies, waits for them, and re-layouts  22.5 us (8%)
  other arithmetic  7.8 us (3%)
  starting transfers between devices  5.48 us (2%)
    all_to_all x1, blocking collectives, shards(): lax.all_to_all(flat_blocks, ('node', 'local'), split_axis=0, concat_axis=...  107 us
    all_to_all x1, waiting for transfers between devices, shards(): lax.all_to_all(computed, ('node', 'local'), split_axis=0, concat_axis=0,...  101 us
    dot_general x1, matrix products, expert(): jnp.dot(hidden, w_down, preferred_element_type=jnp.float32)  17.4 us
    gather x1, local copies, waits for them, and re-layouts, shards(): returned[target].astype(jnp.float32)  10.8 us
    scatter x1, local copies, waits for them, and re-layouts, shards(): jnp.zeros((ep_devices * capacity, model_width), jnp.bfloat16).at[target]  8.17 us
    dot_general x1, matrix products, expert(): gate_part = jnp.dot(inputs, w_gate, preferred_element_type=jnp.float32)  7.11 us
    reduce_sum x1, other arithmetic, shards(): jnp.sum(picked * gate_values.astype(jnp.float32)[:, :, None], axis=1)  5.82 us
    all_to_all x1, starting transfers between devices, shards(): lax.all_to_all(computed, ('node', 'local'), split_axis=0, concat_axis=0,...  5.48 us
  transfers between devices with their start and end apart: 1, of which 1 were waited for; matrix products, arithmetic and copies ran while one was open for 0% of the time, Pallas kernels for 0%

commit v1 on v0

v1 whole, which is shorter than its diff:
```python
import functools

import jax
import jax.numpy as jnp
from jax import lax
from jax.experimental import pallas as pl
from jax.experimental.pallas import tpu as pltpu
from jax.sharding import PartitionSpec as P

CHUNKS = 2
LANES = 128
HIDDEN_TILE = 256
OUT_TILE = 512


def expert_kernel(count, model_width, hidden_steps, *refs):
    pieces = refs[:count]
    pick_ref, gate_ref, up_ref, down_ref, own_ref, other_ref = refs[count : count + 6]
    x_ref, h_ref, g_ref, sems = refs[count + 6 :]
    step = pl.program_id(0)
    rows = pieces[0].shape[0]

    @pl.when(step == 0)
    def _():
        copies = [
            pltpu.make_async_copy(piece, x_ref.at[pl.ds(n * rows, rows)], sems.at[n])
            for n, piece in enumerate(pieces)
        ]
        for copy in copies:
            copy.start()
        for copy in copies:
            copy.wait()
        chosen = x_ref[:, model_width:].astype(jnp.float32) * pick_ref[...]
        g_ref[...] = jnp.broadcast_to(jnp.sum(chosen, axis=1, keepdims=True), g_ref.shape)

    @pl.when(step < hidden_steps)
    def _():
        x = x_ref[:, :model_width]
        gate = jnp.dot(x, gate_ref[...], preferred_element_type=jnp.float32)
        up = jnp.dot(x, up_ref[...], preferred_element_type=jnp.float32)
        width = gate_ref.shape[1]
        h_ref[:, pl.ds(pl.multiple_of(step * width, width), width)] = (
            gate / (1.0 + jnp.exp(-gate)) * up
        ).astype(jnp.bfloat16)

    @pl.when(step >= hidden_steps)
    def _():
        out = jnp.dot(h_ref[...], down_ref[...], preferred_element_type=jnp.float32)
        out = (out * g_ref[:, :1]).astype(jnp.bfloat16)
        half = own_ref.shape[0]
        own_ref[...] = out[:half]
        other_ref[...] = out[half:]


def expert(own, other, pick, w_gate, w_up, w_down):
    pieces = own + other
    count = len(pieces)
    rows = count * pieces[0].shape[0]
    model_width, hidden_width = w_gate.shape
    hidden_steps = hidden_width // HIDDEN_TILE
    out_steps = model_width // OUT_TILE
    hidden_block = pl.BlockSpec(
        (model_width, HIDDEN_TILE), lambda i: (0, jnp.minimum(i, hidden_steps - 1))
    )
    out_block = pl.BlockSpec(
        (rows // 2, OUT_TILE), lambda i: (0, jnp.maximum(i - hidden_steps, 0))
    )
    result = jax.ShapeDtypeStruct((rows // 2, model_width), jnp.bfloat16)
    return pl.pallas_call(
        functools.partial(expert_kernel, count, model_width, hidden_steps),
        grid=(hidden_steps + out_steps,),
        in_specs=[pl.BlockSpec(memory_space=pl.ANY)] * count
        + [
            pl.BlockSpec((1, LANES), lambda i: (0, 0)),
            hidden_block,
            hidden_block,
            pl.BlockSpec(
                (hidden_width, OUT_TILE), lambda i: (0, jnp.maximum(i - hidden_steps, 0))
            ),
        ],
        out_specs=[out_block, out_block],
        out_shape=[result, result],
        scratch_shapes=[
            pltpu.VMEM((rows, pieces[0].shape[1]), jnp.bfloat16),
            pltpu.VMEM((rows, hidden_width), jnp.bfloat16),
            pltpu.VMEM((rows, LANES), jnp.float32),
            pltpu.SemaphoreType.DMA((count,)),
        ],
        compiler_params=pltpu.CompilerParams(
            dimension_semantics=("arbitrary",), vmem_limit_bytes=24 * 1024 * 1024
        ),
        cost_estimate=pl.CostEstimate(
            flops=6 * rows * model_width * hidden_width,
            bytes_accessed=6 * model_width * hidden_width,
            transcendentals=rows * hidden_width,
        ),
        name="expert",
    )(*pieces, pick, w_gate, w_up, w_down)


def ring_of(count):
    order = list(range(0, count, 2)) + list(range(count - 1, 0, -2))
    return [(order[i], order[(i + 1) % count]) for i in range(count)]


def shards(tokens, routes, gate_values, gate_weight, up_weight, down_weight):
    tok_count, model_width = tokens.shape
    nodes = lax.axis_size("node")
    locals_ = lax.axis_size("local")
    slots = nodes * locals_
    half = nodes // 2
    core = lax.axis_index("local")
    me = lax.axis_index("node") * locals_ + core
    ring = ring_of(nodes)
    back = [(b, a) for a, b in ring]
    split = [(locals_ * a, locals_ * b) for a, b in ring] + [
        (locals_ * a + 1, locals_ * b + 1) for a, b in back
    ]
    both = ("node", "local")

    def onward(v):
        return lax.ppermute(v, "node", ring)

    def backward(v):
        return lax.ppermute(v, "node", back)

    def swap(v):
        return lax.ppermute(v, "local", [(0, 1), (1, 0)])

    wide = jnp.arange(LANES, dtype=jnp.int32)
    dense = jnp.sum(
        jnp.where(
            routes[:, :, None] == wide[None, None, :],
            gate_values.astype(jnp.float32)[:, :, None],
            0.0,
        ),
        axis=1,
    ).astype(jnp.bfloat16)
    pick = (wide == me).astype(jnp.float32)[None, :]
    packed = jnp.concatenate([tokens, dense], axis=1)
    size = tok_count // CHUNKS
    weights = (gate_weight[0], up_weight[0], down_weight[0])

    gathered = []
    for chunk in range(CHUNKS):
        mine = packed[chunk * size : (chunk + 1) * size]
        ahead, behind = {0: mine}, {0: mine}
        for d in range(1, half):
            ahead[d] = onward(ahead[d - 1])
            behind[d] = backward(behind[d - 1])
        far = lax.ppermute(jnp.where(core == 0, ahead[half - 1], behind[half - 1]), both, split)
        order = [("far", far), ("mine", mine)]
        for d in range(half - 1, 0, -1):
            order += [(("a", d), ahead[d]), (("b", d), behind[d])]
        gathered.append(order)

    outs = []
    for order in gathered:
        part = {}
        for start in range(0, len(order), 4):
            group = order[start : start + 4]
            own = [v for _, v in group]
            y_own, y_other = expert(own, [swap(v) for v in own], pick, *weights)
            y_swapped = swap(y_other)
            for n, (key, _) in enumerate(group):
                cut = slice(n * size, (n + 1) * size)
                part[key] = y_own[cut].astype(jnp.float32) + y_swapped[cut].astype(jnp.float32)
        narrow = jnp.bfloat16
        got = lax.ppermute(part["far"].astype(narrow), both, split).astype(jnp.float32)
        up_in = jnp.where(core == 0, got, 0.0)
        down_in = jnp.where(core == 0, 0.0, got)
        for d in range(half - 1, 0, -1):
            up_in = onward((part["b", d] + up_in).astype(narrow)).astype(jnp.float32)
            down_in = backward((part["a", d] + down_in).astype(narrow)).astype(jnp.float32)
        outs.append((part["mine"] + up_in + down_in).astype(narrow))
    return jnp.concatenate(outs, axis=0)


def solution(mesh):
    return jax.shard_map(
        shards,
        mesh=mesh,
        in_specs=(
            P(("group", "node", "local"), None),
            P(("group", "node", "local"), None),
            P(("group", "node", "local"), None),
            P(("node", "local"), None, None),
            P(("node", "local"), None, None),
            P(("node", "local"), None, None),
        ),
        out_specs=P(("group", "node", "local"), None),
        check_vma=False,
    )
```

time: 269 us -> 159 us (0.59)
  the two profiles are of different devices: /device:TPU:13 before, /device:TPU:0 now
where the time goes in v1:
time: 159 us
  waiting for transfers between devices  54.4 us (34%)
  Pallas kernels  53.4 us (34%)
  starting transfers between devices  36.8 us (23%)
  local copies, waits for them, and re-layouts  10.8 us (7%)
  other arithmetic  3.57 us (2%)
    pallas_call x4, Pallas kernels, expert(): pl.pallas_call(functools.partial(expert_kernel, count, model_width, hidde...  53.4 us
    ppermute x12, waiting for transfers between devices, onward(): return lax.ppermute(v, 'node', ring)  33.3 us
    ppermute x12, starting transfers between devices, onward(): return lax.ppermute(v, 'node', ring)  22.7 us
    ppermute x12, waiting for transfers between devices, backward(): return lax.ppermute(v, 'node', back)  15.8 us
    unnamed x11, local copies, waits for them, and re-layouts  10 us
    ppermute x20, starting transfers between devices, swap(): return lax.ppermute(v, 'local', [(0, 1), (1, 0)])  4.07 us
    ppermute x12, starting transfers between devices, backward(): return lax.ppermute(v, 'node', back)  3.56 us
    ppermute x2, starting transfers between devices, shards(): lax.ppermute(part['far'].astype(narrow), both, split).astype(jnp.float32)  3.26 us
  transfers between devices with their start and end apart: 48, of which 19 were waited for; matrix products, arithmetic and copies ran while one was open for 1% of the time, Pallas kernels for 34%

profile of v1, /device:TPU:0, one launch (start us, length us, event | category | flops | bytes accessed | tf_op | source)
XLA Modules:
  0.0 159.1 jit_solution(15648649356949104633)
XLA Ops:
  2.8 3.1 %collective-permute-start = (bf16[32,3712]{1,0:T(8,128)(2,1)S(1)}, bf16[32,3712]{1,0:T(8,128)(2,1)S(1)}, u32[]{:S(2)}, u32[]{:S(2)}) collective-permute-start(bf16[32,3712]{1,0:T(8,128)(2,1)S(1)} %get-tuple-element.29.refs_1_), channel_id=1, source_target_pairs={{0,4},{4,8},{8,12},{12,14},{14,10},{10,6},{6,2},{2,0},{1,5},{5,9},... | collective-permute-start | bytes 712712 | tf_op jit(solution)/shard_map/ppermute | solution.py:122
  8.0 4.5 %collective-permute-done.refs_2_ = bf16[32,3712]{1,0:T(8,128)(2,1)S(1)} collective-permute-done((bf16[32,3712]{1,0:T(8,128)(2,1)S(1)}, bf16[32,3712]{1,0:T(8,128)(2,1)S(1)}, u32[]{:S(2)}, u32[]{:S(2)}) %collective-permute-start) | collective-permute-done | bytes 237600 | tf_op jit(solution)/shard_map/ppermute | solution.py:122
  12.5 2.1 %collective-permute-start.1 = (bf16[32,3712]{1,0:T(8,128)(2,1)S(1)}, bf16[32,3712]{1,0:T(8,128)(2,1)S(1)}, u32[]{:S(2)}, u32[]{:S(2)}) collective-permute-start(bf16[32,3712]{1,0:T(8,128)(2,1)S(1)} %collective-permute-done.refs_2_), channel_id=1, source_target_pairs={{0,4},{4,8},{8,12},{12,14},{14,10},{10,6},{6,2},{2,0},{1,5},{5,9},... | collective-permute-start | bytes 712712 | tf_op jit(solution)/shard_map/ppermute | solution.py:122
  14.6 2.9 %collective-permute-done.24.refs_2_ = bf16[32,3712]{1,0:T(8,128)(2,1)S(1)} collective-permute-done((bf16[32,3712]{1,0:T(8,128)(2,1)S(1)}, bf16[32,3712]{1,0:T(8,128)(2,1)S(1)}, u32[]{:S(2)}, u32[]{:S(2)}) %collective-permute-start.24) | collective-permute-done | bytes 237600 | tf_op jit(solution)/shard_map/ppermute | solution.py:122
  19.7 2.9 %collective-permute-done.1.refs_0_ = bf16[32,3712]{1,0:T(8,128)(2,1)S(1)} collective-permute-done((bf16[32,3712]{1,0:T(8,128)(2,1)S(1)}, bf16[32,3712]{1,0:T(8,128)(2,1)S(1)}, u32[]{:S(2)}, u32[]{:S(2)}) %collective-permute-start.1) | collective-permute-done | bytes 237600 | tf_op jit(solution)/shard_map/ppermute | solution.py:122
  24.9 2.9 %collective-permute-done.25.refs_0_ = bf16[32,3712]{1,0:T(8,128)(2,1)S(1)} collective-permute-done((bf16[32,3712]{1,0:T(8,128)(2,1)S(1)}, bf16[32,3712]{1,0:T(8,128)(2,1)S(1)}, u32[]{:S(2)}, u32[]{:S(2)}) %collective-permute-start.25) | collective-permute-done | bytes 237600 | tf_op jit(solution)/shard_map/ppermute | solution.py:122
  27.7 2.1 %collective-permute-done.28.refs_1_ = bf16[32,3712]{1,0:T(8,128)(2,1)S(1)} collective-permute-done((bf16[32,3712]{1,0:T(8,128)(2,1)S(1)}, bf16[32,3712]{1,0:T(8,128)(2,1)S(1)}, u32[]{:S(2)}, u32[]{:S(2)}) %collective-permute-start.28) | collective-permute-done | bytes 237600 | tf_op jit(solution)/shard_map/ppermute | solution.py:125
  34.1 4.9 %collective-permute-done.26.refs_2_ = bf16[32,3712]{1,0:T(8,128)(2,1)S(1)} collective-permute-done((bf16[32,3712]{1,0:T(8,128)(2,1)S(1)}, bf16[32,3712]{1,0:T(8,128)(2,1)S(1)}, u32[]{:S(2)}, u32[]{:S(2)}) %collective-permute-start.26) | collective-permute-done | bytes 237600 | tf_op jit(solution)/shard_map/ppermute | solution.py:122
  44.0 2.2 %collective-permute-done.6.refs_0_ = bf16[32,3712]{1,0:T(8,128)(2,1)S(1)} collective-permute-done((bf16[32,3712]{1,0:T(8,128)(2,1)S(1)}, bf16[32,3712]{1,0:T(8,128)(2,1)S(1)}, u32[]{:S(2)}, u32[]{:S(2)}) %collective-permute-start.6) | collective-permute-done | bytes 237600 | tf_op jit(solution)/shard_map/ppermute | solution.py:151
  46.3 3.1 %copy-done = bf16[1,3584,1024]{2,1,0:T(8,128)(2,1)S(1)} copy-done((bf16[1,3584,1024]{2,1,0:T(8,128)(2,1)S(1)}, bf16[1,3584,1024]{2,1,0:T(8,128)(2,1)}, u32[]{:S(2)}) %copy-start) | copy-done | bytes 7340056
  49.4 3.1 %copy-done.1 = bf16[1,3584,1024]{2,1,0:T(8,128)(2,1)S(1)} copy-done((bf16[1,3584,1024]{2,1,0:T(8,128)(2,1)S(1)}, bf16[1,3584,1024]{2,1,0:T(8,128)(2,1)}, u32[]{:S(2)}) %copy-start.1) | copy-done | bytes 7340056
  52.5 3.1 %copy-done.2 = bf16[1,1024,3584]{2,1,0:T(8,128)(2,1)S(1)} copy-done((bf16[1,1024,3584]{2,1,0:T(8,128)(2,1)S(1)}, bf16[1,1024,3584]{2,1,0:T(8,128)(2,1)}, u32[]{:S(2)}) %copy-start.2) | copy-done | bytes 7340056
  55.5 13.4 %expert.5 = (bf16[128,3584]{1,0:T(8,128)(2,1)S(1)}, bf16[128,3584]{1,0:T(8,128)(2,1)S(1)}) custom-call(bf16[32,3712]{1,0:T(8,128)(2,1)S(1)} %collective-permute-done.1.refs_0_, bf16[32,3712]{1,0:T(8,128)(2,1)S(1)} %collective-permute-done.4.refs_1_, bf16[32,3712]{1,0:T(8,128)(2,1)S(1)} %collective-permute-done.refs_2_, ...), custom_call_target="tpu_custom_call" | custom-call | flops 5637144576 | bytes 22020096 | tf_op jit(solution)/shard_map/expert/pallas_call | solution.py:69
  70.6 13.3 %expert.4 = (bf16[128,3584]{1,0:T(8,128)(2,1)S(1)}, bf16[128,3584]{1,0:T(8,128)(2,1)S(1)}) custom-call(bf16[32,3712]{1,0:T(8,128)(2,1)S(1)} %collective-permute-done.6.refs_0_, bf16[32,3712]{1,0:T(8,128)(2,1)S(1)} %get-tuple-element.29.refs_1_, bf16[32,3712]{1,0:T(8,128)(2,1)S(1)} %collective-permute-done.2.refs_2_, ...), custom_call_target="tpu_custom_call" | custom-call | flops 5637144576 | bytes 22020096 | tf_op jit(solution)/shard_map/expert/pallas_call | solution.py:69
  85.0 13.3 %expert.6 = (bf16[128,3584]{1,0:T(8,128)(2,1)S(1)}, bf16[128,3584]{1,0:T(8,128)(2,1)S(1)}) custom-call(bf16[32,3712]{1,0:T(8,128)(2,1)S(1)} %collective-permute-done.30.refs_0_, bf16[32,3712]{1,0:T(8,128)(2,1)S(1)} %get-tuple-element.30.refs_1_, bf16[32,3712]{1,0:T(8,128)(2,1)S(1)} %collective-permute-done.26.refs_2_, ...), custom_call_target="tpu_custom_call" | custom-call | flops 5637144576 | bytes 22020096 | tf_op jit(solution)/shard_map/expert/pallas_call | solution.py:69
  99.0 13.4 %expert.7 = (bf16[128,3584]{1,0:T(8,128)(2,1)S(1)}, bf16[128,3584]{1,0:T(8,128)(2,1)S(1)}) custom-call(bf16[32,3712]{1,0:T(8,128)(2,1)S(1)} %collective-permute-done.25.refs_0_, bf16[32,3712]{1,0:T(8,128)(2,1)S(1)} %collective-permute-done.28.refs_1_, bf16[32,3712]{1,0:T(8,128)(2,1)S(1)} %collective-permute-done.24.refs_2_, ...), custom_call_target="tpu_custom_call" | custom-call | flops 5637144576 | bytes 22020096 | tf_op jit(solution)/shard_map/expert/pallas_call | solution.py:69
  115.9 2.7 %collective-permute-done.17 = bf16[32,3584]{1,0:T(8,128)(2,1)S(1)} collective-permute-done((bf16[32,3584]{1,0:T(8,128)(2,1)S(1)}, bf16[32,3584]{1,0:T(8,128)(2,1)S(1)}, u32[]{:S(2)}, u32[]{:S(2)}) %collective-permute-start.17) | collective-permute-done | bytes 229408 | tf_op jit(solution)/shard_map/ppermute | solution.py:169
  123.4 4.0 %collective-permute-done.18 = bf16[32,3584]{1,0:T(8,128)(2,1)S(1)} collective-permute-done((bf16[32,3584]{1,0:T(8,128)(2,1)S(1)}, bf16[32,3584]{1,0:T(8,128)(2,1)S(1)}, u32[]{:S(2)}, u32[]{:S(2)}) %collective-permute-start.18) | collective-permute-done | bytes 229408 | tf_op jit(solution)/shard_map/ppermute | solution.py:122
  129.1 3.2 %collective-permute-done.42 = bf16[32,3584]{1,0:T(8,128)(2,1)S(1)} collective-permute-done((bf16[32,3584]{1,0:T(8,128)(2,1)S(1)}, bf16[32,3584]{1,0:T(8,128)(2,1)S(1)}, u32[]{:S(2)}, u32[]{:S(2)}) %collective-permute-start.42) | collective-permute-done | bytes 229408 | tf_op jit(solution)/shard_map/ppermute | solution.py:122
  134.0 3.2 %collective-permute-done.19 = bf16[32,3584]{1,0:T(8,128)(2,1)S(1)} collective-permute-done((bf16[32,3584]{1,0:T(8,128)(2,1)S(1)}, bf16[32,3584]{1,0:T(8,128)(2,1)S(1)}, u32[]{:S(2)}, u32[]{:S(2)}) %collective-permute-start.19) | collective-permute-done | bytes 229408 | tf_op jit(solution)/shard_map/ppermute | solution.py:122
  139.5 2.7 %collective-permute-done.43 = bf16[32,3584]{1,0:T(8,128)(2,1)S(1)} collective-permute-done((bf16[32,3584]{1,0:T(8,128)(2,1)S(1)}, bf16[32,3584]{1,0:T(8,128)(2,1)S(1)}, u32[]{:S(2)}, u32[]{:S(2)}) %collective-permute-start.43) | collective-permute-done | bytes 229408 | tf_op jit(solution)/shard_map/ppermute | solution.py:122
  145.3 5.6 %collective-permute-done.46 = bf16[32,3584]{1,0:T(8,128)(2,1)S(1)} collective-permute-done((bf16[32,3584]{1,0:T(8,128)(2,1)S(1)}, bf16[32,3584]{1,0:T(8,128)(2,1)S(1)}, u32[]{:S(2)}, u32[]{:S(2)}) %collective-permute-start.46) | collective-permute-done | bytes 229408 | tf_op jit(solution)/shard_map/ppermute | solution.py:125
  151.6 4.2 %collective-permute-done.23 = bf16[32,3584]{1,0:T(8,128)(2,1)S(1)} collective-permute-done((bf16[32,3584]{1,0:T(8,128)(2,1)S(1)}, bf16[32,3584]{1,0:T(8,128)(2,1)S(1)}, u32[]{:S(2)}, u32[]{:S(2)}) %collective-permute-start.23) | collective-permute-done | bytes 229408 | tf_op jit(solution)/shard_map/ppermute | solution.py:125
  155.9 2.3 %collective-permute-done.47 = bf16[32,3584]{1,0:T(8,128)(2,1)S(1)} collective-permute-done((bf16[32,3584]{1,0:T(8,128)(2,1)S(1)}, bf16[32,3584]{1,0:T(8,128)(2,1)S(1)}, u32[]{:S(2)}, u32[]{:S(2)}) %collective-permute-start.47) | collective-permute-done | bytes 229408 | tf_op jit(solution)/shard_map/ppermute | solution.py:125
  (107 shorter events, 40.6 us)
Async XLA Ops:
  24.8 17.0 %collective-permute-start.14 = (bf16[32,3712]{1,0:T(8,128)(2,1)S(1)}, bf16[32,3712]{1,0:T(8,128)(2,1)S(1)}, u32[]{:S(2)}, u32[]{:S(2)}) collective-permute-start(bf16[32,3712]{1,0:T(8,128)(2,1)S(1)} %collective-permute-done.refs_2_), channel_id=1, source_target_pairs={{0,1},{1,0},{2,3},{3,2},{4,5},{5,4},{6,7},{7,6},{8,9},{9,8},{10,11... | collective-permute-start | bytes 712712 | tf_op jit(solution)/shard_map/ppermute | solution.py:128
  27.7 14.1 %collective-permute-start.15 = (bf16[32,3712]{1,0:T(8,128)(2,1)S(1)}, bf16[32,3712]{1,0:T(8,128)(2,1)S(1)}, u32[]{:S(2)}, u32[]{:S(2)}) collective-permute-start(bf16[32,3712]{1,0:T(8,128)(2,1)S(1)} %collective-permute-done.3.refs_3_), channel_id=1, source_target_pairs={{0,1},{1,0},{2,3},{3,2},{4,5},{5,4},{6,7},{7,6},{8,9},{9,8},{10,11... | collective-permute-start | bytes 712712 | tf_op jit(solution)/shard_map/ppermute | solution.py:128
  29.9 13.6 %collective-permute-start.12 = (bf16[32,3712]{1,0:T(8,128)(2,1)S(1)}, bf16[32,3712]{1,0:T(8,128)(2,1)S(1)}, u32[]{:S(2)}, u32[]{:S(2)}) collective-permute-start(bf16[32,3712]{1,0:T(8,128)(2,1)S(1)} %collective-permute-done.1.refs_0_), channel_id=1, source_target_pairs={{0,1},{1,0},{2,3},{3,2},{4,5},{5,4},{6,7},{7,6},{8,9},{9,8},{10,11... | collective-permute-start | bytes 712712 | tf_op jit(solution)/shard_map/ppermute | solution.py:128
  41.8 27.1 %collective-permute-start.8 = (bf16[32,3712]{1,0:T(8,128)(2,1)S(1)}, bf16[32,3712]{1,0:T(8,128)(2,1)S(1)}, u32[]{:S(2)}, u32[]{:S(2)}) collective-permute-start(bf16[32,3712]{1,0:T(8,128)(2,1)S(1)} %get-tuple-element.29.refs_1_), channel_id=1, source_target_pairs={{0,1},{1,0},{2,3},{3,2},{4,5},{5,4},{6,7},{7,6},{8,9},{9,8},{10,11... | collective-permute-start | bytes 712712 | tf_op jit(solution)/shard_map/ppermute | solution.py:128
  41.9 28.1 %collective-permute-start.30 = (bf16[32,3712]{1,0:T(8,128)(2,1)S(1)}, bf16[32,3712]{1,0:T(8,128)(2,1)S(1)}, u32[]{:S(2)}, u32[]{:S(2)}) collective-permute-start(bf16[32,3712]{1,0:T(8,128)(2,1)S(1)} %broadcast_select_fusion), channel_id=1, source_target_pairs={{0,4},{4,8},{8,12},{12,14},{14,10},{10,6},{6,2},{2,0},{5,1},{9,5},... | collective-permute-start | bytes 712712 | tf_op jit(solution)/shard_map/ppermute | solution.py:151
  43.5 26.0 %collective-permute-start.10 = (bf16[32,3712]{1,0:T(8,128)(2,1)S(1)}, bf16[32,3712]{1,0:T(8,128)(2,1)S(1)}, u32[]{:S(2)}, u32[]{:S(2)}) collective-permute-start(bf16[32,3712]{1,0:T(8,128)(2,1)S(1)} %collective-permute-done.5.refs_3_), channel_id=1, source_target_pairs={{0,1},{1,0},{2,3},{3,2},{4,5},{5,4},{6,7},{7,6},{8,9},{9,8},{10,11... | collective-permute-start | bytes 712712 | tf_op jit(solution)/shard_map/ppermute | solution.py:128
  43.5 26.1 %collective-permute-start.9 = (bf16[32,3712]{1,0:T(8,128)(2,1)S(1)}, bf16[32,3712]{1,0:T(8,128)(2,1)S(1)}, u32[]{:S(2)}, u32[]{:S(2)}) collective-permute-start(bf16[32,3712]{1,0:T(8,128)(2,1)S(1)} %collective-permute-done.2.refs_2_), channel_id=1, source_target_pairs={{0,1},{1,0},{2,3},{3,2},{4,5},{5,4},{6,7},{7,6},{8,9},{9,8},{10,11... | collective-permute-start | bytes 712712 | tf_op jit(solution)/shard_map/ppermute | solution.py:128
  46.3 23.8 %collective-permute-start.7 = (bf16[32,3712]{1,0:T(8,128)(2,1)S(1)}, bf16[32,3712]{1,0:T(8,128)(2,1)S(1)}, u32[]{:S(2)}, u32[]{:S(2)}) collective-permute-start(bf16[32,3712]{1,0:T(8,128)(2,1)S(1)} %collective-permute-done.6.refs_0_), channel_id=1, source_target_pairs={{0,1},{1,0},{2,3},{3,2},{4,5},{5,4},{6,7},{7,6},{8,9},{9,8},{10,11... | collective-permute-start | bytes 712712 | tf_op jit(solution)/shard_map/ppermute | solution.py:128
  68.9 15.0 %collective-permute-start.32 = (bf16[32,3712]{1,0:T(8,128)(2,1)S(1)}, bf16[32,3712]{1,0:T(8,128)(2,1)S(1)}, u32[]{:S(2)}, u32[]{:S(2)}) collective-permute-start(bf16[32,3712]{1,0:T(8,128)(2,1)S(1)} %get-tuple-element.30.refs_1_), channel_id=1, source_target_pairs={{0,1},{1,0},{2,3},{3,2},{4,5},{5,4},{6,7},{7,6},{8,9},{9,8},{10,11... | collective-permute-start | bytes 712712 | tf_op jit(solution)/shard_map/ppermute | solution.py:128
  69.5 28.9 %collective-permute-start.38 = (bf16[32,3712]{1,0:T(8,128)(2,1)S(1)}, bf16[32,3712]{1,0:T(8,128)(2,1)S(1)}, u32[]{:S(2)}, u32[]{:S(2)}) collective-permute-start(bf16[32,3712]{1,0:T(8,128)(2,1)S(1)} %collective-permute-done.24.refs_2_), channel_id=1, source_target_pairs={{0,1},{1,0},{2,3},{3,2},{4,5},{5,4},{6,7},{7,6},{8,9},{9,8},{10,11... | collective-permute-start | bytes 712712 | tf_op jit(solution)/shard_map/ppermute | solution.py:128
  69.6 14.5 %collective-permute-start.33 = (bf16[32,3712]{1,0:T(8,128)(2,1)S(1)}, bf16[32,3712]{1,0:T(8,128)(2,1)S(1)}, u32[]{:S(2)}, u32[]{:S(2)}) collective-permute-start(bf16[32,3712]{1,0:T(8,128)(2,1)S(1)} %collective-permute-done.26.refs_2_), channel_id=1, source_target_pairs={{0,1},{1,0},{2,3},{3,2},{4,5},{5,4},{6,7},{7,6},{8,9},{9,8},{10,11... | collective-permute-start | bytes 712712 | tf_op jit(solution)/shard_map/ppermute | solution.py:128
  70.0 14.5 %collective-permute-start.34 = (bf16[32,3712]{1,0:T(8,128)(2,1)S(1)}, bf16[32,3712]{1,0:T(8,128)(2,1)S(1)}, u32[]{:S(2)}, u32[]{:S(2)}) collective-permute-start(bf16[32,3712]{1,0:T(8,128)(2,1)S(1)} %collective-permute-done.29.refs_3_), channel_id=1, source_target_pairs={{0,1},{1,0},{2,3},{3,2},{4,5},{5,4},{6,7},{7,6},{8,9},{9,8},{10,11... | collective-permute-start | bytes 712712 | tf_op jit(solution)/shard_map/ppermute | solution.py:128
  70.1 14.5 %collective-permute-start.31 = (bf16[32,3712]{1,0:T(8,128)(2,1)S(1)}, bf16[32,3712]{1,0:T(8,128)(2,1)S(1)}, u32[]{:S(2)}, u32[]{:S(2)}) collective-permute-start(bf16[32,3712]{1,0:T(8,128)(2,1)S(1)} %collective-permute-done.30.refs_0_), channel_id=1, source_target_pairs={{0,1},{1,0},{2,3},{3,2},{4,5},{5,4},{6,7},{7,6},{8,9},{9,8},{10,11... | collective-permute-start | bytes 712712 | tf_op jit(solution)/shard_map/ppermute | solution.py:128
  83.9 14.6 %collective-permute-start.39 = (bf16[32,3712]{1,0:T(8,128)(2,1)S(1)}, bf16[32,3712]{1,0:T(8,128)(2,1)S(1)}, u32[]{:S(2)}, u32[]{:S(2)}) collective-permute-start(bf16[32,3712]{1,0:T(8,128)(2,1)S(1)} %collective-permute-done.27.refs_3_), channel_id=1, source_target_pairs={{0,1},{1,0},{2,3},{3,2},{4,5},{5,4},{6,7},{7,6},{8,9},{9,8},{10,11... | collective-permute-start | bytes 712712 | tf_op jit(solution)/shard_map/ppermute | solution.py:128
  84.1 14.9 %collective-permute-start.36 = (bf16[32,3712]{1,0:T(8,128)(2,1)S(1)}, bf16[32,3712]{1,0:T(8,128)(2,1)S(1)}, u32[]{:S(2)}, u32[]{:S(2)}) collective-permute-start(bf16[32,3712]{1,0:T(8,128)(2,1)S(1)} %collective-permute-done.25.refs_0_), channel_id=1, source_target_pairs={{0,1},{1,0},{2,3},{3,2},{4,5},{5,4},{6,7},{7,6},{8,9},{9,8},{10,11... | collective-permute-start | bytes 712712 | tf_op jit(solution)/shard_map/ppermute | solution.py:128
  84.5 14.5 %collective-permute-start.37 = (bf16[32,3712]{1,0:T(8,128)(2,1)S(1)}, bf16[32,3712]{1,0:T(8,128)(2,1)S(1)}, u32[]{:S(2)}, u32[]{:S(2)}) collective-permute-start(bf16[32,3712]{1,0:T(8,128)(2,1)S(1)} %collective-permute-done.28.refs_1_), channel_id=1, source_target_pairs={{0,1},{1,0},{2,3},{3,2},{4,5},{5,4},{6,7},{7,6},{8,9},{9,8},{10,11... | collective-permute-start | bytes 712712 | tf_op jit(solution)/shard_map/ppermute | solution.py:128
  84.6 27.9 %collective-permute-start.11 = (bf16[128,3584]{1,0:T(8,128)(2,1)S(1)}, bf16[128,3584]{1,0:T(8,128)(2,1)S(1)}, u32[]{:S(2)}, u32[]{:S(2)}) collective-permute-start(bf16[128,3584]{1,0:T(8,128)(2,1)S(1)} %get-tuple-element.14), channel_id=1, source_target_pairs={{0,1},{1,0},{2,3},{3,2},{4,5},{5,4},{6,7},{7,6},{8,9},{9,8},{10,11... | collective-permute-start | bytes 2752520 | tf_op jit(solution)/shard_map/ppermute | solution.py:128
  98.4 24.5 %collective-permute-start.16 = (bf16[128,3584]{1,0:T(8,128)(2,1)S(1)}, bf16[128,3584]{1,0:T(8,128)(2,1)S(1)}, u32[]{:S(2)}, u32[]{:S(2)}) collective-permute-start(bf16[128,3584]{1,0:T(8,128)(2,1)S(1)} %get-tuple-element.16), channel_id=1, source_target_pairs={{0,1},{1,0},{2,3},{3,2},{4,5},{5,4},{6,7},{7,6},{8,9},{9,8},{10,11... | collective-permute-start | bytes 2752520 | tf_op jit(solution)/shard_map/ppermute | solution.py:128
  98.5 15.6 %collective-permute-start.35 = (bf16[128,3584]{1,0:T(8,128)(2,1)S(1)}, bf16[128,3584]{1,0:T(8,128)(2,1)S(1)}, u32[]{:S(2)}, u32[]{:S(2)}) collective-permute-start(bf16[128,3584]{1,0:T(8,128)(2,1)S(1)} %get-tuple-element.18), channel_id=1, source_target_pairs={{0,1},{1,0},{2,3},{3,2},{4,5},{5,4},{6,7},{7,6},{8,9},{9,8},{10,11... | collective-permute-start | bytes 2752520 | tf_op jit(solution)/shard_map/ppermute | solution.py:128
  112.3 16.8 %collective-permute-start.40 = (bf16[128,3584]{1,0:T(8,128)(2,1)S(1)}, bf16[128,3584]{1,0:T(8,128)(2,1)S(1)}, u32[]{:S(2)}, u32[]{:S(2)}) collective-permute-start(bf16[128,3584]{1,0:T(8,128)(2,1)S(1)} %get-tuple-element.20), channel_id=1, source_target_pairs={{0,1},{1,0},{2,3},{3,2},{4,5},{5,4},{6,7},{7,6},{8,9},{9,8},{10,11... | collective-permute-start | bytes 2752520 | tf_op jit(solution)/shard_map/ppermute | solution.py:128
  120.4 13.6 %collective-permute-start.21 = (bf16[32,3584]{1,0:T(8,128)(2,1)S(1)}, bf16[32,3584]{1,0:T(8,128)(2,1)S(1)}, u32[]{:S(2)}, u32[]{:S(2)}) collective-permute-start(bf16[32,3584]{1,0:T(8,128)(2,1)S(1)} %get-tuple-element.22), channel_id=1, source_target_pairs={{4,0},{8,4},{12,8},{14,12},{10,14},{6,10},{2,6},{0,2},{5,1},{9,5},... | collective-permute-start | bytes 688136 | tf_op jit(solution)/shard_map/ppermute | solution.py:125
  122.9 16.6 %collective-permute-start.45 = (bf16[32,3584]{1,0:T(8,128)(2,1)S(1)}, bf16[32,3584]{1,0:T(8,128)(2,1)S(1)}, u32[]{:S(2)}, u32[]{:S(2)}) collective-permute-start(bf16[32,3584]{1,0:T(8,128)(2,1)S(1)} %get-tuple-element.24), channel_id=1, source_target_pairs={{4,0},{8,4},{12,8},{14,12},{10,14},{6,10},{2,6},{0,2},{5,1},{9,5},... | collective-permute-start | bytes 688136 | tf_op jit(solution)/shard_map/ppermute | solution.py:125
  138.0 13.6 %collective-permute-start.20 = (bf16[32,3584]{1,0:T(8,128)(2,1)S(1)}, bf16[32,3584]{1,0:T(8,128)(2,1)S(1)}, u32[]{:S(2)}, u32[]{:S(2)}) collective-permute-start(bf16[32,3584]{1,0:T(8,128)(2,1)S(1)} %get-tuple-element.25), channel_id=1, source_target_pairs={{0,4},{4,8},{8,12},{12,14},{14,10},{10,6},{6,2},{2,0},{1,5},{5,9},... | collective-permute-start | bytes 688136 | tf_op jit(solution)/shard_map/ppermute | solution.py:122
  142.9 13.0 %collective-permute-start.44 = (bf16[32,3584]{1,0:T(8,128)(2,1)S(1)}, bf16[32,3584]{1,0:T(8,128)(2,1)S(1)}, u32[]{:S(2)}, u32[]{:S(2)}) collective-permute-start(bf16[32,3584]{1,0:T(8,128)(2,1)S(1)} %get-tuple-element.27), channel_id=1, source_target_pairs={{0,4},{4,8},{8,12},{12,14},{14,10},{10,6},{6,2},{2,0},{1,5},{5,9},... | collective-permute-start | bytes 688136 | tf_op jit(solution)/shard_map/ppermute | solution.py:122
  (29 other events, 265.7 us)

commit v2 on v0

v2 whole, which is shorter than its diff:
```python
import functools

import jax
import jax.numpy as jnp
from jax import lax
from jax.experimental import pallas as pl
from jax.experimental.pallas import tpu as pltpu
from jax.sharding import PartitionSpec as P

PARTS = 2
LANES = 128
HIDDEN_TILE = 512
OUT_TILE = 896


def expert_kernel(count, loads, *refs):
    pieces, refs = refs[:count], refs[count:]
    pick_ref, *sources, own_ref, other_ref = refs[:6]
    if loads:
        *kept, h_ref, sems = refs[6:]
    else:
        kept, (h_ref,) = sources, refs[6:]
    gate_ref, up_ref, down_ref = kept
    model_width, hidden_width = gate_ref.shape
    hidden_cuts = [pl.ds(s, HIDDEN_TILE) for s in range(0, hidden_width, HIDDEN_TILE)]
    out_cuts = [pl.ds(s, OUT_TILE) for s in range(0, model_width, OUT_TILE)]
    order = [(which, cut) for cut in hidden_cuts for which in (0, 1)]
    order += [(2, cut) for cut in out_cuts]
    copies = []
    if loads:
        for n, (which, cut) in enumerate(order):
            copies.append(
                pltpu.make_async_copy(
                    sources[which].at[:, cut], kept[which].at[:, cut], sems.at[n]
                )
            )
            copies[n].start()

    def ready():
        if copies:
            copies.pop(0).wait()

    def rows(start, size):
        return jnp.concatenate([p[:, start : start + size] for p in pieces], axis=0)

    chosen = rows(model_width, LANES).astype(jnp.float32) * pick_ref[...]
    weight = jnp.sum(chosen, axis=1, keepdims=True)
    for cut in hidden_cuts:
        x = rows(0, model_width)
        ready()
        gate = jnp.dot(x, gate_ref[:, cut], preferred_element_type=jnp.float32)
        ready()
        up = jnp.dot(x, up_ref[:, cut], preferred_element_type=jnp.float32)
        h_ref[:, cut] = (gate / (1.0 + jnp.exp(-gate)) * up).astype(jnp.bfloat16)
    half = own_ref.shape[0]
    for cut in out_cuts:
        ready()
        out = jnp.dot(h_ref[...], down_ref[:, cut], preferred_element_type=jnp.float32)
        out = (out * weight).astype(jnp.bfloat16)
        own_ref[:, cut] = out[:half]
        other_ref[:, cut] = out[half:]


def expert(own, other, pick, weights, source="hbm", keep=False):
    loads = source == "hbm"
    pieces = own + other
    count = len(pieces)
    rows = count * pieces[0].shape[0]
    model_width, hidden_width = weights[0].shape
    result = jax.ShapeDtypeStruct((rows // 2, model_width), jnp.bfloat16)
    vmem = pl.BlockSpec(memory_space=pltpu.VMEM)
    held = [pltpu.VMEM(w.shape, w.dtype) for w in weights]
    scratch = [pltpu.VMEM((rows, hidden_width), jnp.bfloat16)]
    out_shape = [result, result]
    limit = 16
    if loads:
        steps = 2 * (hidden_width // HIDDEN_TILE) + model_width // OUT_TILE
        scratch.append(pltpu.SemaphoreType.DMA((steps,)))
        if keep:
            out_shape += held
        else:
            scratch = held + scratch
            limit += 22
    space = pltpu.HBM if loads else pltpu.VMEM
    weights = [pltpu.with_memory_space_constraint(w, space) for w in weights]
    return pl.pallas_call(
        functools.partial(expert_kernel, count, loads),
        in_specs=[vmem] * (count + 1)
        + [pl.BlockSpec(memory_space=pl.ANY if loads else pltpu.VMEM)] * 3,
        out_specs=[vmem] * len(out_shape),
        out_shape=out_shape,
        scratch_shapes=scratch,
        compiler_params=pltpu.CompilerParams(vmem_limit_bytes=limit * 1024 * 1024),
        cost_estimate=pl.CostEstimate(
            flops=6 * rows * model_width * hidden_width,
            bytes_accessed=6 * model_width * hidden_width if loads else 0,
            transcendentals=rows * hidden_width,
        ),
        name="expert",
    )(*pieces, pick, *weights)


def ring_of(count):
    order = list(range(0, count, 2)) + list(range(count - 1, 0, -2))
    return [(order[i], order[(i + 1) % count]) for i in range(count)]


def shards(tokens, routes, gate_values, gate_weight, up_weight, down_weight):
    tok_count, model_width = tokens.shape
    nodes = lax.axis_size("node")
    locals_ = lax.axis_size("local")
    slots = nodes * locals_
    half = nodes // 2
    core = lax.axis_index("local")
    me = lax.axis_index("node") * locals_ + core
    ring = ring_of(nodes)
    back = [(b, a) for a, b in ring]
    split = [(locals_ * a, locals_ * b) for a, b in ring] + [
        (locals_ * a + 1, locals_ * b + 1) for a, b in back
    ]
    both = ("node", "local")

    def onward(v):
        return lax.ppermute(v, "node", ring)

    def backward(v):
        return lax.ppermute(v, "node", back)

    def swap(v):
        return lax.ppermute(v, "local", [(0, 1), (1, 0)])

    wide = jnp.arange(LANES, dtype=jnp.int32)
    dense = jnp.sum(
        jnp.where(
            routes[:, :, None] == wide[None, None, :],
            gate_values.astype(jnp.float32)[:, :, None],
            0.0,
        ),
        axis=1,
    ).astype(jnp.bfloat16)
    pick = (wide == me).astype(jnp.float32)[None, :]
    packed = jnp.concatenate([tokens, dense], axis=1)
    size = tok_count // PARTS
    weights = (gate_weight[0], up_weight[0], down_weight[0])

    narrow = jnp.bfloat16

    def tie(values, *after):
        return lax.optimization_barrier((values, after))[0]

    def run(own, *how):
        y_own, y_other, *held = expert(own, [swap(v) for v in own], pick, *how)
        y_swapped = swap(y_other)

        def total(n, part):
            cut = slice((n * PARTS + part) * size, (n * PARTS + part + 1) * size)
            return y_own[cut].astype(jnp.float32) + y_swapped[cut].astype(jnp.float32)

        return total, y_own, held

    mine_sum, token, held = run([packed], weights, "hbm", True)
    ahead, behind, near = [packed], [packed], {}
    for d in range(1, half):
        ahead.append(onward(ahead[-1]))
        behind.append(backward(behind[-1]))
        ahead[d], behind[d] = tie((ahead[d], behind[d]), token)
        if d < half - 1:
            how = (held, "vmem") if d % 2 else (weights, "hbm", True)
            near[d], token, fresh = run([ahead[d], behind[d]], *how)
            held = fresh or held
    far = lax.ppermute(jnp.where(core == 0, ahead[-1], behind[-1]), both, split)
    near[half - 1], token, _ = run([ahead[-1], behind[-1]], held, "vmem")
    far_sum, _, _ = run([tie(far, token)], held, "vmem")

    sums = [far_sum(0, part).astype(narrow) for part in range(PARTS)]
    got = [lax.ppermute(v, both, split).astype(jnp.float32) for v in sums]
    up_in = [jnp.where(core == 0, v, 0.0) for v in got]
    down_in = [jnp.where(core == 0, 0.0, v) for v in got]
    before = sums[-1]
    for d in range(half - 1, 0, -1):
        for part in range(PARTS):
            up, down = tie((up_in[part], down_in[part]), before)
            up = (near[d](1, part) + up).astype(narrow)
            down = (near[d](0, part) + down).astype(narrow)
            before = up
            up_in[part] = onward(up).astype(jnp.float32)
            down_in[part] = backward(down).astype(jnp.float32)
    outs = [
        (mine_sum(0, part) + up_in[part] + down_in[part]).astype(narrow) for part in range(PARTS)
    ]
    return jnp.concatenate(outs, axis=0)


def solution(mesh):
    return jax.shard_map(
        shards,
        mesh=mesh,
        in_specs=(
            P(("group", "node", "local"), None),
            P(("group", "node", "local"), None),
            P(("group", "node", "local"), None),
            P(("node", "local"), None, None),
            P(("node", "local"), None, None),
            P(("node", "local"), None, None),
        ),
        out_specs=P(("group", "node", "local"), None),
        check_vma=False,
    )
```

time: 269 us -> 109 us (0.41)
  the two profiles are of different devices: /device:TPU:13 before, /device:TPU:0 now
where the time goes in v2:
time: 109 us
  waiting for transfers between devices  42.7 us (39%)
  Pallas kernels  33.6 us (31%)
  starting transfers between devices  25.4 us (23%)
  other arithmetic  3.8 us (3%)
  local copies, waits for them, and re-layouts  3.24 us (3%)
    pallas_call x5, Pallas kernels, expert(): pl.pallas_call(functools.partial(expert_kernel, count, loads), in_specs=[...  33.6 us
    ppermute x9, waiting for transfers between devices, backward(): return lax.ppermute(v, 'node', back)  19.3 us
    ppermute x9, starting transfers between devices, onward(): return lax.ppermute(v, 'node', ring)  15.1 us
    ppermute x9, waiting for transfers between devices, onward(): return lax.ppermute(v, 'node', ring)  13 us
    ppermute x2, waiting for transfers between devices, shards(): got = [lax.ppermute(v, both, split).astype(jnp.float32) for v in sums]  5.93 us
    ppermute x9, starting transfers between devices, backward(): return lax.ppermute(v, 'node', back)  3.95 us
    ppermute x13, waiting for transfers between devices, swap(): return lax.ppermute(v, 'local', [(0, 1), (1, 0)])  3.92 us
    ppermute x13, starting transfers between devices, swap(): return lax.ppermute(v, 'local', [(0, 1), (1, 0)])  2.77 us
  transfers between devices with their start and end apart: 34, of which 21 were waited for; matrix products, arithmetic and copies ran while one was open for 1% of the time, Pallas kernels for 28%

profile of v2, /device:TPU:0, one launch (start us, length us, event | category | flops | bytes accessed | tf_op | source)
XLA Modules:
  0.0 109.0 jit_solution(5010085474308655430)
XLA Ops:
  3.3 2.6 %collective-permute-start.2 = (bf16[64,3712]{1,0:T(8,128)(2,1)S(1)}, bf16[64,3712]{1,0:T(8,128)(2,1)S(1)}, u32[]{:S(2)}, u32[]{:S(2)}) collective-permute-start(bf16[64,3712]{1,0:T(8,128)(2,1)S(1)} %pad_maximum_fusion.refs_0_), channel_id=1, source_target_pairs={{0,4},{4,8},{8,12},{12,14},{14,10},{10,6},{6,2},{2,0},{1,5},{5,9},... | collective-permute-start | bytes 1425416 | tf_op jit(solution)/shard_map/ppermute | solution.py:124
  6.0 7.9 %expert.5 = (bf16[64,3584]{1,0:T(8,128)(2,1)S(1)}, bf16[64,3584]{1,0:T(8,128)(2,1)S(1)}, bf16[3584,1024]{1,0:T(8,128)(2,1)S(1)}, bf16[3584,1024]{1,0:T(8,128)(2,1)S(1)}, bf16[1024,3584]{1,0:T(8,128)(2,1)S(1)}) custom-call(bf16[64,3712]{1,0:T(8,128)(2,1)S(1)} %pad_maximum_fusion.refs_0_, bf16[64,3712]{1,0:T(8,128)(2,1)S(1)} %collective-permute-done.refs_1_, ...), custom_call_target="tpu_custom_call" | custom-call | flops 2818572288 | bytes 22020096 | tf_op jit(solution)/shard_map/expert/pallas_call | solution.py:86
  14.7 2.7 %collective-permute-done.2.refs_0_ = bf16[64,3712]{1,0:T(8,128)(2,1)S(1)} collective-permute-done((bf16[64,3712]{1,0:T(8,128)(2,1)S(1)}, bf16[64,3712]{1,0:T(8,128)(2,1)S(1)}, u32[]{:S(2)}, u32[]{:S(2)}) %collective-permute-start.2) | collective-permute-done | bytes 475168 | tf_op jit(solution)/shard_map/ppermute | solution.py:124
  19.4 1.6 %collective-permute-start.7 = (bf16[64,3712]{1,0:T(8,128)(2,1)S(1)}, bf16[64,3712]{1,0:T(8,128)(2,1)S(1)}, u32[]{:S(2)}, u32[]{:S(2)}) collective-permute-start(bf16[64,3712]{1,0:T(8,128)(2,1)S(1)} %collective-permute-done.2.refs_0_), channel_id=1, source_target_pairs={{0,4},{4,8},{8,12},{12,14},{14,10},{10,6},{6,2},{2,0},{1,5},{5,9},... | collective-permute-start | bytes 1425416 | tf_op jit(solution)/shard_map/ppermute | solution.py:124
  21.5 6.4 %expert.6 = (bf16[128,3584]{1,0:T(8,128)(2,1)S(1)}, bf16[128,3584]{1,0:T(8,128)(2,1)S(1)}) custom-call(bf16[64,3712]{1,0:T(8,128)(2,1)S(1)} %collective-permute-done.2.refs_0_, bf16[64,3712]{1,0:T(8,128)(2,1)S(1)} %collective-permute-done.3.refs_1_, bf16[64,3712]{1,0:T(8,128)(2,1)S(1)} %collective-permute-done.4.refs_2_, ...), custom_call_target="tpu_custom_call" | custom-call | flops 5637144576 | tf_op jit(solution)/shard_map/expert/pallas_call | solution.py:86
  28.8 3.4 %collective-permute-done.7.refs_0_ = bf16[64,3712]{1,0:T(8,128)(2,1)S(1)} collective-permute-done((bf16[64,3712]{1,0:T(8,128)(2,1)S(1)}, bf16[64,3712]{1,0:T(8,128)(2,1)S(1)}, u32[]{:S(2)}, u32[]{:S(2)}) %collective-permute-start.7) | collective-permute-done | bytes 475168 | tf_op jit(solution)/shard_map/ppermute | solution.py:124
  34.0 1.6 %collective-permute-start.12 = (bf16[64,3712]{1,0:T(8,128)(2,1)S(1)}, bf16[64,3712]{1,0:T(8,128)(2,1)S(1)}, u32[]{:S(2)}, u32[]{:S(2)}) collective-permute-start(bf16[64,3712]{1,0:T(8,128)(2,1)S(1)} %collective-permute-done.7.refs_0_), channel_id=1, source_target_pairs={{0,4},{4,8},{8,12},{12,14},{14,10},{10,6},{6,2},{2,0},{1,5},{5,9},... | collective-permute-start | bytes 1425416 | tf_op jit(solution)/shard_map/ppermute | solution.py:124
  36.0 9.8 %expert.7 = (bf16[128,3584]{1,0:T(8,128)(2,1)S(1)}, bf16[128,3584]{1,0:T(8,128)(2,1)S(1)}, bf16[3584,1024]{1,0:T(8,128)(2,1)S(1)}, bf16[3584,1024]{1,0:T(8,128)(2,1)S(1)}, bf16[1024,3584]{1,0:T(8,128)(2,1)S(1)}) custom-call(bf16[64,3712]{1,0:T(8,128)(2,1)S(1)} %collective-permute-done.7.refs_0_, bf16[64,3712]{1,0:T(8,128)(2,1)S(1)} %collective-permute-done.8.refs_1_, ...), custom_call_target="tpu_custom_call" | custom-call | flops 5637144576 | bytes 22020096 | tf_op jit(solution)/shard_map/expert/pallas_call | solution.py:86
  48.7 1.6 %collective-permute-start.17 = (bf16[64,3712]{1,0:T(8,128)(2,1)S(1)}, bf16[64,3712]{1,0:T(8,128)(2,1)S(1)}, u32[]{:S(2)}, u32[]{:S(2)}) collective-permute-start(bf16[64,3712]{1,0:T(8,128)(2,1)S(1)} %broadcast_select_fusion), channel_id=1, source_target_pairs={{0,4},{4,8},{8,12},{12,14},{14,10},{10,6},{6,2},{2,0},{5,1},{9,5},... | collective-permute-start | bytes 1425416 | tf_op jit(solution)/shard_map/ppermute | solution.py:171
  50.6 6.3 %expert.8 = (bf16[128,3584]{1,0:T(8,128)(2,1)S(1)}, bf16[128,3584]{1,0:T(8,128)(2,1)S(1)}) custom-call(bf16[64,3712]{1,0:T(8,128)(2,1)S(1)} %collective-permute-done.12.refs_0_, bf16[64,3712]{1,0:T(8,128)(2,1)S(1)} %collective-permute-done.13.refs_1_, bf16[64,3712]{1,0:T(8,128)(2,1)S(1)} %collective-permute-done.14.refs_2_, ...), custom_call_target="tpu_custom_call" | custom-call | flops 5637144576 | tf_op jit(solution)/shard_map/expert/pallas_call | solution.py:86
  57.4 1.8 %collective-permute-done.18.refs_1_ = bf16[64,3712]{1,0:T(8,128)(2,1)S(1)} collective-permute-done((bf16[64,3712]{1,0:T(8,128)(2,1)S(1)}, bf16[64,3712]{1,0:T(8,128)(2,1)S(1)}, u32[]{:S(2)}, u32[]{:S(2)}) %collective-permute-start.18) | collective-permute-done | bytes 475168 | tf_op jit(solution)/shard_map/ppermute | solution.py:130
  59.2 3.3 %expert.9 = (bf16[64,3584]{1,0:T(8,128)(2,1)S(1)}, bf16[64,3584]{1,0:T(8,128)(2,1)S(1)}) custom-call(bf16[64,3712]{1,0:T(8,128)(2,1)S(1)} %collective-permute-done.17.refs_0_, bf16[64,3712]{1,0:T(8,128)(2,1)S(1)} %collective-permute-done.18.refs_1_, f32[1,128]{1,0:T(1,128)S(1)} %compare_convert_fusion.refs_2_.refs_4_, ...), custom_call_target="tpu_custom_call" | custom-call | flops 2818572288 | tf_op jit(solution)/shard_map/expert/pallas_call | solution.py:86
  62.7 1.7 %collective-permute-done.19 = bf16[64,3584]{1,0:T(8,128)(2,1)S(1)} collective-permute-done((bf16[64,3584]{1,0:T(8,128)(2,1)S(1)}, bf16[64,3584]{1,0:T(8,128)(2,1)S(1)}, u32[]{:S(2)}, u32[]{:S(2)}) %collective-permute-start.19) | collective-permute-done | bytes 458784 | tf_op jit(solution)/shard_map/ppermute | solution.py:130
  67.0 3.5 %collective-permute-done.20 = bf16[32,3584]{1,0:T(8,128)(2,1)S(1)} collective-permute-done((bf16[32,3584]{1,0:T(8,128)(2,1)S(1)}, bf16[32,3584]{1,0:T(8,128)(2,1)S(1)}, u32[]{:S(2)}, u32[]{:S(2)}) %collective-permute-start.20) | collective-permute-done | bytes 229408 | tf_op jit(solution)/shard_map/ppermute | solution.py:176
  70.6 2.4 %collective-permute-done.23 = bf16[32,3584]{1,0:T(8,128)(2,1)S(1)} collective-permute-done((bf16[32,3584]{1,0:T(8,128)(2,1)S(1)}, bf16[32,3584]{1,0:T(8,128)(2,1)S(1)}, u32[]{:S(2)}, u32[]{:S(2)}) %collective-permute-start.23) | collective-permute-done | bytes 229408 | tf_op jit(solution)/shard_map/ppermute | solution.py:176
  73.9 1.6 %collective-permute-start.21 = (bf16[32,3584]{1,0:T(8,128)(2,1)S(1)}, bf16[32,3584]{1,0:T(8,128)(2,1)S(1)}, u32[]{:S(2)}, u32[]{:S(2)}) collective-permute-start(bf16[32,3584]{1,0:T(8,128)(2,1)S(1)} %add_convert_fusion.13), channel_id=1, source_target_pairs={{0,4},{4,8},{8,12},{12,14},{14,10},{10,6},{6,2},{2,0},{1,5},{5,9},... | collective-permute-start | bytes 688136 | tf_op jit(solution)/shard_map/ppermute | solution.py:124
  77.5 4.5 %collective-permute-done.22 = bf16[32,3584]{1,0:T(8,128)(2,1)S(1)} collective-permute-done((bf16[32,3584]{1,0:T(8,128)(2,1)S(1)}, bf16[32,3584]{1,0:T(8,128)(2,1)S(1)}, u32[]{:S(2)}, u32[]{:S(2)}) %collective-permute-start.22) | collective-permute-done | bytes 229408 | tf_op jit(solution)/shard_map/ppermute | solution.py:127
  82.5 2.8 %collective-permute-done.26 = bf16[32,3584]{1,0:T(8,128)(2,1)S(1)} collective-permute-done((bf16[32,3584]{1,0:T(8,128)(2,1)S(1)}, bf16[32,3584]{1,0:T(8,128)(2,1)S(1)}, u32[]{:S(2)}, u32[]{:S(2)}) %collective-permute-start.26) | collective-permute-done | bytes 229408 | tf_op jit(solution)/shard_map/ppermute | solution.py:124
  86.3 1.6 %collective-permute-start.24 = (bf16[32,3584]{1,0:T(8,128)(2,1)S(1)}, bf16[32,3584]{1,0:T(8,128)(2,1)S(1)}, u32[]{:S(2)}, u32[]{:S(2)}) collective-permute-start(bf16[32,3584]{1,0:T(8,128)(2,1)S(1)} %add_convert_fusion.10), channel_id=1, source_target_pairs={{0,4},{4,8},{8,12},{12,14},{14,10},{10,6},{6,2},{2,0},{1,5},{5,9},... | collective-permute-start | bytes 688136 | tf_op jit(solution)/shard_map/ppermute | solution.py:124
  87.9 1.6 %collective-permute-start.30 = (bf16[32,3584]{1,0:T(8,128)(2,1)S(1)}, bf16[32,3584]{1,0:T(8,128)(2,1)S(1)}, u32[]{:S(2)}, u32[]{:S(2)}) collective-permute-start(bf16[32,3584]{1,0:T(8,128)(2,1)S(1)} %get-tuple-element.80), channel_id=1, source_target_pairs={{0,4},{4,8},{8,12},{12,14},{14,10},{10,6},{6,2},{2,0},{1,5},{5,9},... | collective-permute-start | bytes 688136 | tf_op jit(solution)/shard_map/ppermute | solution.py:124
  89.9 4.3 %collective-permute-done.25 = bf16[32,3584]{1,0:T(8,128)(2,1)S(1)} collective-permute-done((bf16[32,3584]{1,0:T(8,128)(2,1)S(1)}, bf16[32,3584]{1,0:T(8,128)(2,1)S(1)}, u32[]{:S(2)}, u32[]{:S(2)}) %collective-permute-start.25) | collective-permute-done | bytes 229408 | tf_op jit(solution)/shard_map/ppermute | solution.py:127
  94.3 2.3 %collective-permute-done.30 = bf16[32,3584]{1,0:T(8,128)(2,1)S(1)} collective-permute-done((bf16[32,3584]{1,0:T(8,128)(2,1)S(1)}, bf16[32,3584]{1,0:T(8,128)(2,1)S(1)}, u32[]{:S(2)}, u32[]{:S(2)}) %collective-permute-start.30) | collective-permute-done | bytes 229408 | tf_op jit(solution)/shard_map/ppermute | solution.py:124
  101.1 4.1 %collective-permute-done.29 = bf16[32,3584]{1,0:T(8,128)(2,1)S(1)} collective-permute-done((bf16[32,3584]{1,0:T(8,128)(2,1)S(1)}, bf16[32,3584]{1,0:T(8,128)(2,1)S(1)}, u32[]{:S(2)}, u32[]{:S(2)}) %collective-permute-start.29) | collective-permute-done | bytes 229408 | tf_op jit(solution)/shard_map/ppermute | solution.py:127
  105.5 2.2 %collective-permute-done.33 = bf16[32,3584]{1,0:T(8,128)(2,1)S(1)} collective-permute-done((bf16[32,3584]{1,0:T(8,128)(2,1)S(1)}, bf16[32,3584]{1,0:T(8,128)(2,1)S(1)}, u32[]{:S(2)}, u32[]{:S(2)}) %collective-permute-start.33) | collective-permute-done | bytes 229408 | tf_op jit(solution)/shard_map/ppermute | solution.py:127
  (82 shorter events, 27.2 us)
Async XLA Ops:
  3.3 14.1 %collective-permute-start.2 = (bf16[64,3712]{1,0:T(8,128)(2,1)S(1)}, bf16[64,3712]{1,0:T(8,128)(2,1)S(1)}, u32[]{:S(2)}, u32[]{:S(2)}) collective-permute-start(bf16[64,3712]{1,0:T(8,128)(2,1)S(1)} %pad_maximum_fusion.refs_0_), channel_id=1, source_target_pairs={{0,4},{4,8},{8,12},{12,14},{14,10},{10,6},{6,2},{2,0},{1,5},{5,9},... | collective-permute-start | bytes 1425416 | tf_op jit(solution)/shard_map/ppermute | solution.py:124
  6.0 12.9 %collective-permute-start.3 = (bf16[64,3712]{1,0:T(8,128)(2,1)S(1)}, bf16[64,3712]{1,0:T(8,128)(2,1)S(1)}, u32[]{:S(2)}, u32[]{:S(2)}) collective-permute-start(bf16[64,3712]{1,0:T(8,128)(2,1)S(1)} %pad_maximum_fusion.refs_0_), channel_id=1, source_target_pairs={{4,0},{8,4},{12,8},{14,12},{10,14},{6,10},{2,6},{0,2},{5,1},{9,5},... | collective-permute-start | bytes 1425416 | tf_op jit(solution)/shard_map/ppermute | solution.py:127
  19.4 12.8 %collective-permute-start.7 = (bf16[64,3712]{1,0:T(8,128)(2,1)S(1)}, bf16[64,3712]{1,0:T(8,128)(2,1)S(1)}, u32[]{:S(2)}, u32[]{:S(2)}) collective-permute-start(bf16[64,3712]{1,0:T(8,128)(2,1)S(1)} %collective-permute-done.2.refs_0_), channel_id=1, source_target_pairs={{0,4},{4,8},{8,12},{12,14},{14,10},{10,6},{6,2},{2,0},{1,5},{5,9},... | collective-permute-start | bytes 1425416 | tf_op jit(solution)/shard_map/ppermute | solution.py:124
  21.0 12.5 %collective-permute-start.8 = (bf16[64,3712]{1,0:T(8,128)(2,1)S(1)}, bf16[64,3712]{1,0:T(8,128)(2,1)S(1)}, u32[]{:S(2)}, u32[]{:S(2)}) collective-permute-start(bf16[64,3712]{1,0:T(8,128)(2,1)S(1)} %collective-permute-done.3.refs_1_), channel_id=1, source_target_pairs={{4,0},{8,4},{12,8},{14,12},{10,14},{6,10},{2,6},{0,2},{5,1},{9,5},... | collective-permute-start | bytes 1425416 | tf_op jit(solution)/shard_map/ppermute | solution.py:127
  34.0 12.8 %collective-permute-start.12 = (bf16[64,3712]{1,0:T(8,128)(2,1)S(1)}, bf16[64,3712]{1,0:T(8,128)(2,1)S(1)}, u32[]{:S(2)}, u32[]{:S(2)}) collective-permute-start(bf16[64,3712]{1,0:T(8,128)(2,1)S(1)} %collective-permute-done.7.refs_0_), channel_id=1, source_target_pairs={{0,4},{4,8},{8,12},{12,14},{14,10},{10,6},{6,2},{2,0},{1,5},{5,9},... | collective-permute-start | bytes 1425416 | tf_op jit(solution)/shard_map/ppermute | solution.py:124
  35.6 12.5 %collective-permute-start.13 = (bf16[64,3712]{1,0:T(8,128)(2,1)S(1)}, bf16[64,3712]{1,0:T(8,128)(2,1)S(1)}, u32[]{:S(2)}, u32[]{:S(2)}) collective-permute-start(bf16[64,3712]{1,0:T(8,128)(2,1)S(1)} %collective-permute-done.8.refs_1_), channel_id=1, source_target_pairs={{4,0},{8,4},{12,8},{14,12},{10,14},{6,10},{2,6},{0,2},{5,1},{9,5},... | collective-permute-start | bytes 1425416 | tf_op jit(solution)/shard_map/ppermute | solution.py:127
  48.7 8.7 %collective-permute-start.17 = (bf16[64,3712]{1,0:T(8,128)(2,1)S(1)}, bf16[64,3712]{1,0:T(8,128)(2,1)S(1)}, u32[]{:S(2)}, u32[]{:S(2)}) collective-permute-start(bf16[64,3712]{1,0:T(8,128)(2,1)S(1)} %broadcast_select_fusion), channel_id=1, source_target_pairs={{0,4},{4,8},{8,12},{12,14},{14,10},{10,6},{6,2},{2,0},{5,1},{9,5},... | collective-permute-start | bytes 1425416 | tf_op jit(solution)/shard_map/ppermute | solution.py:171
  66.1 19.4 %collective-permute-start.11 = (bf16[128,3584]{1,0:T(8,128)(2,1)S(1)}, bf16[128,3584]{1,0:T(8,128)(2,1)S(1)}, u32[]{:S(2)}, u32[]{:S(2)}) collective-permute-start(bf16[128,3584]{1,0:T(8,128)(2,1)S(1)} %get-tuple-element.52), channel_id=1, source_target_pairs={{0,1},{1,0},{2,3},{3,2},{4,5},{5,4},{6,7},{7,6},{8,9},{9,8},{10,11... | collective-permute-start | bytes 2752520 | tf_op jit(solution)/shard_map/ppermute | solution.py:130
  66.1 7.0 %collective-permute-start.16 = (bf16[128,3584]{1,0:T(8,128)(2,1)S(1)}, bf16[128,3584]{1,0:T(8,128)(2,1)S(1)}, u32[]{:S(2)}, u32[]{:S(2)}) collective-permute-start(bf16[128,3584]{1,0:T(8,128)(2,1)S(1)} %get-tuple-element.59), channel_id=1, source_target_pairs={{0,1},{1,0},{2,3},{3,2},{4,5},{5,4},{6,7},{7,6},{8,9},{9,8},{10,11... | collective-permute-start | bytes 2752520 | tf_op jit(solution)/shard_map/ppermute | solution.py:130
  66.6 6.5 %collective-permute-start.23 = (bf16[32,3584]{1,0:T(8,128)(2,1)S(1)}, bf16[32,3584]{1,0:T(8,128)(2,1)S(1)}, u32[]{:S(2)}, u32[]{:S(2)}) collective-permute-start(bf16[32,3584]{1,0:T(8,128)(2,1)S(1)} %get-tuple-element.87), channel_id=1, source_target_pairs={{0,4},{4,8},{8,12},{12,14},{14,10},{10,6},{6,2},{2,0},{5,1},{9,5},... | collective-permute-start | bytes 688136 | tf_op jit(solution)/shard_map/ppermute | solution.py:176
  73.4 8.6 %collective-permute-start.22 = (bf16[32,3584]{1,0:T(8,128)(2,1)S(1)}, bf16[32,3584]{1,0:T(8,128)(2,1)S(1)}, u32[]{:S(2)}, u32[]{:S(2)}) collective-permute-start(bf16[32,3584]{1,0:T(8,128)(2,1)S(1)} %get-tuple-element.81), channel_id=1, source_target_pairs={{4,0},{8,4},{12,8},{14,12},{10,14},{6,10},{2,6},{0,2},{5,1},{9,5},... | collective-permute-start | bytes 688136 | tf_op jit(solution)/shard_map/ppermute | solution.py:127
  73.9 8.5 %collective-permute-start.21 = (bf16[32,3584]{1,0:T(8,128)(2,1)S(1)}, bf16[32,3584]{1,0:T(8,128)(2,1)S(1)}, u32[]{:S(2)}, u32[]{:S(2)}) collective-permute-start(bf16[32,3584]{1,0:T(8,128)(2,1)S(1)} %add_convert_fusion.13), channel_id=1, source_target_pairs={{0,4},{4,8},{8,12},{12,14},{14,10},{10,6},{6,2},{2,0},{1,5},{5,9},... | collective-permute-start | bytes 688136 | tf_op jit(solution)/shard_map/ppermute | solution.py:124
  75.5 9.8 %collective-permute-start.26 = (bf16[32,3584]{1,0:T(8,128)(2,1)S(1)}, bf16[32,3584]{1,0:T(8,128)(2,1)S(1)}, u32[]{:S(2)}, u32[]{:S(2)}) collective-permute-start(bf16[32,3584]{1,0:T(8,128)(2,1)S(1)} %get-tuple-element.83), channel_id=1, source_target_pairs={{0,4},{4,8},{8,12},{12,14},{14,10},{10,6},{6,2},{2,0},{1,5},{5,9},... | collective-permute-start | bytes 688136 | tf_op jit(solution)/shard_map/ppermute | solution.py:124
  77.0 8.4 %collective-permute-start.27 = (bf16[32,3584]{1,0:T(8,128)(2,1)S(1)}, bf16[32,3584]{1,0:T(8,128)(2,1)S(1)}, u32[]{:S(2)}, u32[]{:S(2)}) collective-permute-start(bf16[32,3584]{1,0:T(8,128)(2,1)S(1)} %get-tuple-element.82), channel_id=1, source_target_pairs={{4,0},{8,4},{12,8},{14,12},{10,14},{6,10},{2,6},{0,2},{5,1},{9,5},... | collective-permute-start | bytes 688136 | tf_op jit(solution)/shard_map/ppermute | solution.py:127
  82.0 14.7 %collective-permute-start.6 = (bf16[128,3584]{1,0:T(8,128)(2,1)S(1)}, bf16[128,3584]{1,0:T(8,128)(2,1)S(1)}, u32[]{:S(2)}, u32[]{:S(2)}) collective-permute-start(bf16[128,3584]{1,0:T(8,128)(2,1)S(1)} %copy-done.1), channel_id=1, source_target_pairs={{0,1},{1,0},{2,3},{3,2},{4,5},{5,4},{6,7},{7,6},{8,9},{9,8},{10,11... | collective-permute-start | bytes 2752520 | tf_op jit(solution)/shard_map/ppermute | solution.py:130
  85.8 8.4 %collective-permute-start.25 = (bf16[32,3584]{1,0:T(8,128)(2,1)S(1)}, bf16[32,3584]{1,0:T(8,128)(2,1)S(1)}, u32[]{:S(2)}, u32[]{:S(2)}) collective-permute-start(bf16[32,3584]{1,0:T(8,128)(2,1)S(1)} %get-tuple-element.78), channel_id=1, source_target_pairs={{4,0},{8,4},{12,8},{14,12},{10,14},{6,10},{2,6},{0,2},{5,1},{9,5},... | collective-permute-start | bytes 688136 | tf_op jit(solution)/shard_map/ppermute | solution.py:127
  86.3 8.0 %collective-permute-start.24 = (bf16[32,3584]{1,0:T(8,128)(2,1)S(1)}, bf16[32,3584]{1,0:T(8,128)(2,1)S(1)}, u32[]{:S(2)}, u32[]{:S(2)}) collective-permute-start(bf16[32,3584]{1,0:T(8,128)(2,1)S(1)} %add_convert_fusion.10), channel_id=1, source_target_pairs={{0,4},{4,8},{8,12},{12,14},{14,10},{10,6},{6,2},{2,0},{1,5},{5,9},... | collective-permute-start | bytes 688136 | tf_op jit(solution)/shard_map/ppermute | solution.py:124
  87.9 8.7 %collective-permute-start.30 = (bf16[32,3584]{1,0:T(8,128)(2,1)S(1)}, bf16[32,3584]{1,0:T(8,128)(2,1)S(1)}, u32[]{:S(2)}, u32[]{:S(2)}) collective-permute-start(bf16[32,3584]{1,0:T(8,128)(2,1)S(1)} %get-tuple-element.80), channel_id=1, source_target_pairs={{0,4},{4,8},{8,12},{12,14},{14,10},{10,6},{6,2},{2,0},{1,5},{5,9},... | collective-permute-start | bytes 688136 | tf_op jit(solution)/shard_map/ppermute | solution.py:124
  89.4 7.2 %collective-permute-start.31 = (bf16[32,3584]{1,0:T(8,128)(2,1)S(1)}, bf16[32,3584]{1,0:T(8,128)(2,1)S(1)}, u32[]{:S(2)}, u32[]{:S(2)}) collective-permute-start(bf16[32,3584]{1,0:T(8,128)(2,1)S(1)} %get-tuple-element.79), channel_id=1, source_target_pairs={{4,0},{8,4},{12,8},{14,12},{10,14},{6,10},{2,6},{0,2},{5,1},{9,5},... | collective-permute-start | bytes 688136 | tf_op jit(solution)/shard_map/ppermute | solution.py:127
  94.2 6.9 %collective-permute-start.1 = (bf16[64,3584]{1,0:T(8,128)(2,1)S(1)}, bf16[64,3584]{1,0:T(8,128)(2,1)S(1)}, u32[]{:S(2)}, u32[]{:S(2)}) collective-permute-start(bf16[64,3584]{1,0:T(8,128)(2,1)S(1)} %copy-done.3), channel_id=1, source_target_pairs={{0,1},{1,0},{2,3},{3,2},{4,5},{5,4},{6,7},{7,6},{8,9},{9,8},{10,11... | collective-permute-start | bytes 1376264 | tf_op jit(solution)/shard_map/ppermute | solution.py:130
  97.0 8.2 %collective-permute-start.29 = (bf16[32,3584]{1,0:T(8,128)(2,1)S(1)}, bf16[32,3584]{1,0:T(8,128)(2,1)S(1)}, u32[]{:S(2)}, u32[]{:S(2)}) collective-permute-start(bf16[32,3584]{1,0:T(8,128)(2,1)S(1)} %get-tuple-element.75), channel_id=1, source_target_pairs={{4,0},{8,4},{12,8},{14,12},{10,14},{6,10},{2,6},{0,2},{5,1},{9,5},... | collective-permute-start | bytes 688136 | tf_op jit(solution)/shard_map/ppermute | solution.py:127
  97.6 7.9 %collective-permute-start.32 = (bf16[32,3584]{1,0:T(8,128)(2,1)S(1)}, bf16[32,3584]{1,0:T(8,128)(2,1)S(1)}, u32[]{:S(2)}, u32[]{:S(2)}) collective-permute-start(bf16[32,3584]{1,0:T(8,128)(2,1)S(1)} %get-tuple-element.77), channel_id=1, source_target_pairs={{0,4},{4,8},{8,12},{12,14},{14,10},{10,6},{6,2},{2,0},{1,5},{5,9},... | collective-permute-start | bytes 688136 | tf_op jit(solution)/shard_map/ppermute | solution.py:124
  99.1 8.6 %collective-permute-start.33 = (bf16[32,3584]{1,0:T(8,128)(2,1)S(1)}, bf16[32,3584]{1,0:T(8,128)(2,1)S(1)}, u32[]{:S(2)}, u32[]{:S(2)}) collective-permute-start(bf16[32,3584]{1,0:T(8,128)(2,1)S(1)} %get-tuple-element.76), channel_id=1, source_target_pairs={{4,0},{8,4},{12,8},{14,12},{10,14},{6,10},{2,6},{0,2},{5,1},{9,5},... | collective-permute-start | bytes 688136 | tf_op jit(solution)/shard_map/ppermute | solution.py:127
  99.6 8.3 %collective-permute-start.28 = (bf16[32,3584]{1,0:T(8,128)(2,1)S(1)}, bf16[32,3584]{1,0:T(8,128)(2,1)S(1)}, u32[]{:S(2)}, u32[]{:S(2)}) collective-permute-start(bf16[32,3584]{1,0:T(8,128)(2,1)S(1)} %add_convert_fusion.6), channel_id=1, source_target_pairs={{0,4},{4,8},{8,12},{12,14},{14,10},{10,6},{6,2},{2,0},{1,5},{5,9},... | collective-permute-start | bytes 688136 | tf_op jit(solution)/shard_map/ppermute | solution.py:124
  (14 other events, 78.8 us)

commit v3 on v2

--- a/solution.py
+++ b/solution.py
@@ -72,7 +72,7 @@
     held = [pltpu.VMEM(w.shape, w.dtype) for w in weights]
     scratch = [pltpu.VMEM((rows, hidden_width), jnp.bfloat16)]
     out_shape = [result, result]
-    limit = 16
+    limit = 8
     if loads:
         steps = 2 * (hidden_width // HIDDEN_TILE) + model_width // OUT_TILE
         scratch.append(pltpu.SemaphoreType.DMA((steps,)))
@@ -100,6 +100,89 @@
     )(*pieces, pick, *weights)
 
 
+def add_kernel(cuts, mine_ref, other_ref, *refs):
+    count = len(cuts)
+    for cut, in_ref, out_ref in zip(cuts, refs[:count], refs[-count:]):
+        total = mine_ref[cut, :].astype(jnp.float32) + other_ref[cut, :].astype(jnp.float32)
+        out_ref[...] = (total + in_ref[...].astype(jnp.float32)).astype(out_ref.dtype)
+
+
+def add(cuts, mine, other, received, after):
+    vmem = pl.BlockSpec(memory_space=pltpu.VMEM)
+    count = len(cuts)
+    return pl.pallas_call(
+        functools.partial(add_kernel, cuts),
+        in_specs=[vmem] * (2 + count) + [pl.BlockSpec(memory_space=pl.ANY)],
+        out_specs=[vmem] * count,
+        out_shape=[jax.ShapeDtypeStruct(v.shape, v.dtype) for v in received],
+        compiler_params=pltpu.CompilerParams(vmem_limit_bytes=4 * 1024 * 1024),
+        cost_estimate=pl.CostEstimate(
+            flops=2 * count * received[0].size, bytes_accessed=0, transcendentals=0
+        ),
+        name="add",
+    )(mine, other, *received, after)
+
+
+def pack_kernel(tokens_ref, routes_ref, gates_ref, out_ref, sem):
+    model_width = tokens_ref.shape[1]
+    copy = pltpu.make_async_copy(tokens_ref, out_ref.at[:, pl.ds(0, model_width)], sem)
+    copy.start()
+    top_count, count = routes_ref.shape
+    slot = lax.broadcasted_iota(jnp.int32, (LANES, count), 0)
+    gates = gates_ref[...].astype(jnp.float32)
+    dense = jnp.zeros((LANES, count), jnp.float32)
+    for k in range(top_count):
+        dense += jnp.where(routes_ref[k : k + 1, :] == slot, gates[k : k + 1, :], 0.0)
+    same = lax.broadcasted_iota(jnp.int32, (count, count), 0) == lax.broadcasted_iota(
+        jnp.int32, (count, count), 1
+    )
+    turned = lax.dot_general(
+        jnp.where(same, 1.0, 0.0).astype(jnp.bfloat16),
+        dense.astype(jnp.bfloat16),
+        (((1,), (1,)), ((), ())),
+        preferred_element_type=jnp.float32,
+    )
+    out_ref[:, model_width:] = turned.astype(jnp.bfloat16)
+    copy.wait()
+
+
+def pack(tokens, routes, gate_values):
+    vmem = pl.BlockSpec(memory_space=pltpu.VMEM)
+    count, model_width = tokens.shape
+    return pl.pallas_call(
+        pack_kernel,
+        in_specs=[pl.BlockSpec(memory_space=pl.ANY), vmem, vmem],
+        out_specs=vmem,
+        out_shape=jax.ShapeDtypeStruct((count, model_width + LANES), jnp.bfloat16),
+        scratch_shapes=[pltpu.SemaphoreType.DMA],
+        compiler_params=pltpu.CompilerParams(vmem_limit_bytes=4 * 1024 * 1024),
+        name="pack",
+    )(*[pltpu.with_memory_space_constraint(v, pltpu.HBM) for v in (tokens, routes.T, gate_values.T)])
+
+
+def finish_kernel(mine_ref, other_ref, *refs):
+    *received, out_ref = refs
+    size = received[0].shape[0]
+    for part in range(len(received) // 2):
+        cut = slice(part * size, (part + 1) * size)
+        total = mine_ref[cut, :].astype(jnp.float32) + other_ref[cut, :].astype(jnp.float32)
+        for ref in received[2 * part : 2 * part + 2]:
+            total += ref[...].astype(jnp.float32)
+        out_ref[cut, :] = total.astype(out_ref.dtype)
+
+
+def finish(mine, other, received):
+    vmem = pl.BlockSpec(memory_space=pltpu.VMEM)
+    return pl.pallas_call(
+        finish_kernel,
+        in_specs=[vmem] * (2 + len(received)),
+        out_specs=vmem,
+        out_shape=jax.ShapeDtypeStruct(mine.shape, mine.dtype),
+        compiler_params=pltpu.CompilerParams(vmem_limit_bytes=8 * 1024 * 1024),
+        name="finish",
+    )(mine, other, *received)
+
+
 def ring_of(count):
     order = list(range(0, count, 2)) + list(range(count - 1, 0, -2))
     return [(order[i], order[(i + 1) % count]) for i in range(count)]
@@ -130,16 +213,8 @@
         return lax.ppermute(v, "local", [(0, 1), (1, 0)])
 
     wide = jnp.arange(LANES, dtype=jnp.int32)
-    dense = jnp.sum(
-        jnp.where(
-            routes[:, :, None] == wide[None, None, :],
-            gate_values.astype(jnp.float32)[:, :, None],
-            0.0,
-        ),
-        axis=1,
-    ).astype(jnp.bfloat16)
     pick = (wide == me).astype(jnp.float32)[None, :]
-    packed = jnp.concatenate([tokens, dense], axis=1)
+    packed = pack(tokens, routes, gate_values)
     size = tok_count // PARTS
     weights = (gate_weight[0], up_weight[0], down_weight[0])
 
@@ -153,42 +228,54 @@
         y_swapped = swap(y_other)
 
         def total(n, part):
-            cut = slice((n * PARTS + part) * size, (n * PARTS + part + 1) * size)
+            cut = slice(n * tok_count + part * size, n * tok_count + (part + 1) * size)
             return y_own[cut].astype(jnp.float32) + y_swapped[cut].astype(jnp.float32)
 
-        return total, y_own, held
-
-    mine_sum, token, held = run([packed], weights, "hbm", True)
+        def added(part, received, after):
+            cuts = [
+                slice(n * tok_count + part * size, n * tok_count + (part + 1) * size)
+                for n in range(len(received))
+            ]
+            return add(cuts, y_own, y_swapped, received, after)
+
+        def finished(received):
+            return finish(y_own, y_swapped, received)
+
+        return (total, added, finished), y_own, held
+
+    def plan(d):
+        return (held, "vmem") if d % 2 else (weights, "hbm", True)
+
     ahead, behind, near = [packed], [packed], {}
+    ahead.append(onward(packed))
+    behind.append(backward(packed))
+    mine_sum, token, held = run([packed], *plan(0))
     for d in range(1, half):
-        ahead.append(onward(ahead[-1]))
-        behind.append(backward(behind[-1]))
         ahead[d], behind[d] = tie((ahead[d], behind[d]), token)
         if d < half - 1:
-            how = (held, "vmem") if d % 2 else (weights, "hbm", True)
-            near[d], token, fresh = run([ahead[d], behind[d]], *how)
-            held = fresh or held
-    far = lax.ppermute(jnp.where(core == 0, ahead[-1], behind[-1]), both, split)
-    near[half - 1], token, _ = run([ahead[-1], behind[-1]], held, "vmem")
+            ahead.append(onward(ahead[d]))
+            behind.append(backward(behind[d]))
+        else:
+            far = lax.ppermute(jnp.where(core == 0, ahead[d], behind[d]), both, split)
+        near[d], token, fresh = run([ahead[d], behind[d]], *plan(d))
+        held = fresh or held
     far_sum, _, _ = run([tie(far, token)], held, "vmem")
 
-    sums = [far_sum(0, part).astype(narrow) for part in range(PARTS)]
-    got = [lax.ppermute(v, both, split).astype(jnp.float32) for v in sums]
-    up_in = [jnp.where(core == 0, v, 0.0) for v in got]
-    down_in = [jnp.where(core == 0, 0.0, v) for v in got]
+    sums = [far_sum[0](0, part).astype(narrow) for part in range(PARTS)]
+    got = [lax.ppermute(v, both, split) for v in sums]
+    up_in, down_in = [None] * PARTS, [None] * PARTS
     before = sums[-1]
     for d in range(half - 1, 0, -1):
         for part in range(PARTS):
-            up, down = tie((up_in[part], down_in[part]), before)
-            up = (near[d](1, part) + up).astype(narrow)
-            down = (near[d](0, part) + down).astype(narrow)
+            if d == half - 1:
+                up_in[part] = jnp.where(core == 0, got[part], 0)
+                down_in[part] = jnp.where(core == 0, 0, got[part])
+            down, up = near[d][1](part, [down_in[part], up_in[part]], before)
             before = up
-            up_in[part] = onward(up).astype(jnp.float32)
-            down_in[part] = backward(down).astype(jnp.float32)
-    outs = [
-        (mine_sum(0, part) + up_in[part] + down_in[part]).astype(narrow) for part in range(PARTS)
-    ]
-    return jnp.concatenate(outs, axis=0)
+            up_in[part] = onward(up)
+            down_in[part] = backward(down)
+    received = [v for part in range(PARTS) for v in (up_in[part], down_in[part])]
+    return mine_sum[2](received)
 
 
 def solution(mesh):

time: 109 us -> 103 us (0.945)
  waiting for transfers between devices: 42.7 us -> 37.4 us
  Pallas kernels: 33.6 us -> 37.4 us
  other arithmetic: 3.8 us -> 0.23 us
  local copies, waits for them, and re-layouts: 3.24 us -> 1.72 us
    ppermute x9, waiting for transfers between devices: 19.3 us -> 14 us  [backward(): return lax.ppermute(v, 'node', back)]
    pallas_call x0 -> x8, Pallas kernels: none -> 3.72 us  [the longest x1 1.73 us: pack(): pl.pallas_call(pack_kernel, in_specs=[pl.BlockSpec(memory_space=pl.ANY),...]
    ppermute x3, waiting for transfers between devices: 6.42 us -> 4.13 us  [the longest x2 3.74 us: shards(): got = [lax.ppermute(v, both, split) for v in sums]]
    ppermute x9, waiting for transfers between devices: 13 us -> 15.3 us  [onward(): return lax.ppermute(v, 'node', ring)]
    concatenate x2 -> x0, other arithmetic: 1.85 us -> none  [the longest x1 1.05 us: shards(): packed = jnp.concatenate([tokens, dense], axis=1)]
    convert_element_type x16 -> x1, other arithmetic: 1.54 us -> 0.11 us  [shards(): sums = [far_sum[0](0, part).astype(narrow) for part in range(PARTS)]]
    unnamed x9 -> x8, local copies, waits for them, and re-layouts: 2.48 us -> 1.72 us
  transfers between devices with their start and end apart: 34 -> 34, of which waited for: 21 -> 23; matrix products, arithmetic and copies ran while one was open for 1% -> 0% of each run, Pallas kernels for 28% -> 31%
where the time goes in v3:
time: 103 us; the launch traced here: 102 us
  Pallas kernels  37.4 us (36%)
  waiting for transfers between devices  37.4 us (36%)
  starting transfers between devices  25.6 us (25%)
  local copies, waits for them, and re-layouts  1.72 us (2%)
    pallas_call x5, Pallas kernels, expert(): pl.pallas_call(functools.partial(expert_kernel, count, loads), in_specs=[...  33.6 us
    ppermute x9, starting transfers between devices, onward(): return lax.ppermute(v, 'node', ring)  15.4 us
    ppermute x9, waiting for transfers between devices, onward(): return lax.ppermute(v, 'node', ring)  15.3 us
    ppermute x9, waiting for transfers between devices, backward(): return lax.ppermute(v, 'node', back)  14 us
    ppermute x13, waiting for transfers between devices, swap(): return lax.ppermute(v, 'local', [(0, 1), (1, 0)])  3.92 us
    ppermute x9, starting transfers between devices, backward(): return lax.ppermute(v, 'node', back)  3.83 us
    ppermute x2, waiting for transfers between devices, shards(): got = [lax.ppermute(v, both, split) for v in sums]  3.74 us
    ppermute x13, starting transfers between devices, swap(): return lax.ppermute(v, 'local', [(0, 1), (1, 0)])  2.77 us
  transfers between devices with their start and end apart: 34, of which 23 were waited for; matrix products, arithmetic and copies ran while one was open for 0% of the time, Pallas kernels for 31%

profile of v3, /device:TPU:0, one launch (start us, length us, event | category | flops | bytes accessed | tf_op | source)
XLA Modules:
  0.0 102.4 jit_solution(2183274238428959282)
XLA Ops:
  0.0 1.7 %pack.1.refs_0_ = bf16[64,3712]{1,0:T(8,128)(2,1)S(1)} custom-call(bf16[64,3584]{1,0:T(8,128)(2,1)} %tokens_ref.1, s32[8,64]{1,0:T(8,128)} %bitcast.11, bf16[8,64]{1,0:T(8,128)(2,1)} %bitcast.12), custom_call_target="tpu_custom_call" | custom-call | tf_op jit(solution)/shard_map/pack/pallas_call | solution.py:152
  2.3 2.6 %collective-permute-start.2 = (bf16[64,3712]{1,0:T(8,128)(2,1)S(1)}, bf16[64,3712]{1,0:T(8,128)(2,1)S(1)}, u32[]{:S(2)}, u32[]{:S(2)}) collective-permute-start(bf16[64,3712]{1,0:T(8,128)(2,1)S(1)} %pack.1.refs_0_), channel_id=1, source_target_pairs={{0,4},{4,8},{8,12},{12,14},{14,10},{10,6},{6,2},{2,0},{1,5},{5,9},... | collective-permute-start | bytes 1425416 | tf_op jit(solution)/shard_map/ppermute | solution.py:207
  4.9 7.9 %expert.5 = (bf16[64,3584]{1,0:T(8,128)(2,1)S(1)}, bf16[64,3584]{1,0:T(8,128)(2,1)S(1)}, bf16[3584,1024]{1,0:T(8,128)(2,1)S(1)}, bf16[3584,1024]{1,0:T(8,128)(2,1)S(1)}, bf16[1024,3584]{1,0:T(8,128)(2,1)S(1)}) custom-call(bf16[64,3712]{1,0:T(8,128)(2,1)S(1)} %pack.1.refs_0_, bf16[64,3712]{1,0:T(8,128)(2,1)S(1)} %collective-permute-done.refs_1_, ...), custom_call_target="tpu_custom_call" | custom-call | flops 2818572288 | bytes 22020096 | tf_op jit(solution)/shard_map/expert/pallas_call | solution.py:86
  13.6 2.7 %collective-permute-done.2.refs_0_ = bf16[64,3712]{1,0:T(8,128)(2,1)S(1)} collective-permute-done((bf16[64,3712]{1,0:T(8,128)(2,1)S(1)}, bf16[64,3712]{1,0:T(8,128)(2,1)S(1)}, u32[]{:S(2)}, u32[]{:S(2)}) %collective-permute-start.2) | collective-permute-done | bytes 475168 | tf_op jit(solution)/shard_map/ppermute | solution.py:207
  18.3 1.6 %collective-permute-start.7 = (bf16[64,3712]{1,0:T(8,128)(2,1)S(1)}, bf16[64,3712]{1,0:T(8,128)(2,1)S(1)}, u32[]{:S(2)}, u32[]{:S(2)}) collective-permute-start(bf16[64,3712]{1,0:T(8,128)(2,1)S(1)} %collective-permute-done.2.refs_0_), channel_id=1, source_target_pairs={{0,4},{4,8},{8,12},{12,14},{14,10},{10,6},{6,2},{2,0},{1,5},{5,9},... | collective-permute-start | bytes 1425416 | tf_op jit(solution)/shard_map/ppermute | solution.py:207
  20.4 6.4 %expert.6 = (bf16[128,3584]{1,0:T(8,128)(2,1)S(1)}, bf16[128,3584]{1,0:T(8,128)(2,1)S(1)}) custom-call(bf16[64,3712]{1,0:T(8,128)(2,1)S(1)} %collective-permute-done.2.refs_0_, bf16[64,3712]{1,0:T(8,128)(2,1)S(1)} %collective-permute-done.3.refs_1_, bf16[64,3712]{1,0:T(8,128)(2,1)S(1)} %collective-permute-done.4.refs_2_, ...), custom_call_target="tpu_custom_call" | custom-call | flops 5637144576 | tf_op jit(solution)/shard_map/expert/pallas_call | solution.py:86
  27.8 3.4 %collective-permute-done.7.refs_0_ = bf16[64,3712]{1,0:T(8,128)(2,1)S(1)} collective-permute-done((bf16[64,3712]{1,0:T(8,128)(2,1)S(1)}, bf16[64,3712]{1,0:T(8,128)(2,1)S(1)}, u32[]{:S(2)}, u32[]{:S(2)}) %collective-permute-start.7) | collective-permute-done | bytes 475168 | tf_op jit(solution)/shard_map/ppermute | solution.py:207
  35.0 9.7 %expert.7 = (bf16[128,3584]{1,0:T(8,128)(2,1)S(1)}, bf16[128,3584]{1,0:T(8,128)(2,1)S(1)}, bf16[3584,1024]{1,0:T(8,128)(2,1)S(1)}, bf16[3584,1024]{1,0:T(8,128)(2,1)S(1)}, bf16[1024,3584]{1,0:T(8,128)(2,1)S(1)}) custom-call(bf16[64,3712]{1,0:T(8,128)(2,1)S(1)} %collective-permute-done.7.refs_0_, bf16[64,3712]{1,0:T(8,128)(2,1)S(1)} %collective-permute-done.8.refs_1_, ...), custom_call_target="tpu_custom_call" | custom-call | flops 5637144576 | bytes 22020096 | tf_op jit(solution)/shard_map/expert/pallas_call | solution.py:86
  49.5 6.4 %expert.8 = (bf16[128,3584]{1,0:T(8,128)(2,1)S(1)}, bf16[128,3584]{1,0:T(8,128)(2,1)S(1)}) custom-call(bf16[64,3712]{1,0:T(8,128)(2,1)S(1)} %collective-permute-done.12.refs_0_, bf16[64,3712]{1,0:T(8,128)(2,1)S(1)} %collective-permute-done.13.refs_1_, bf16[64,3712]{1,0:T(8,128)(2,1)S(1)} %collective-permute-done.14.refs_2_, ...), custom_call_target="tpu_custom_call" | custom-call | flops 5637144576 | tf_op jit(solution)/shard_map/expert/pallas_call | solution.py:86
  56.3 1.8 %collective-permute-done.18.refs_1_ = bf16[64,3712]{1,0:T(8,128)(2,1)S(1)} collective-permute-done((bf16[64,3712]{1,0:T(8,128)(2,1)S(1)}, bf16[64,3712]{1,0:T(8,128)(2,1)S(1)}, u32[]{:S(2)}, u32[]{:S(2)}) %collective-permute-start.18) | collective-permute-done | bytes 475168 | tf_op jit(solution)/shard_map/ppermute | solution.py:213
  58.1 3.2 %expert.9 = (bf16[64,3584]{1,0:T(8,128)(2,1)S(1)}, bf16[64,3584]{1,0:T(8,128)(2,1)S(1)}) custom-call(bf16[64,3712]{1,0:T(8,128)(2,1)S(1)} %collective-permute-done.17.refs_0_, bf16[64,3712]{1,0:T(8,128)(2,1)S(1)} %collective-permute-done.18.refs_1_, f32[1,128]{1,0:T(1,128)S(1)} %compare_convert_fusion.refs_2_.refs_4_, ...), custom_call_target="tpu_custom_call" | custom-call | flops 2818572288 | tf_op jit(solution)/shard_map/expert/pallas_call | solution.py:86
  61.6 1.7 %collective-permute-done.19 = bf16[64,3584]{1,0:T(8,128)(2,1)S(1)} collective-permute-done((bf16[64,3584]{1,0:T(8,128)(2,1)S(1)}, bf16[64,3584]{1,0:T(8,128)(2,1)S(1)}, u32[]{:S(2)}, u32[]{:S(2)}) %collective-permute-start.19) | collective-permute-done | bytes 458784 | tf_op jit(solution)/shard_map/ppermute | solution.py:213
  65.9 3.5 %collective-permute-done.20 = bf16[32,3584]{1,0:T(8,128)(2,1)S(1)} collective-permute-done((bf16[32,3584]{1,0:T(8,128)(2,1)S(1)}, bf16[32,3584]{1,0:T(8,128)(2,1)S(1)}, u32[]{:S(2)}, u32[]{:S(2)}) %collective-permute-start.20) | collective-permute-done | bytes 229408 | tf_op jit(solution)/shard_map/ppermute | solution.py:265
  70.2 1.6 %collective-permute-start.22 = (bf16[32,3584]{1,0:T(8,128)(2,1)S(1)}, bf16[32,3584]{1,0:T(8,128)(2,1)S(1)}, u32[]{:S(2)}, u32[]{:S(2)}) collective-permute-start(bf16[32,3584]{1,0:T(8,128)(2,1)S(1)} %get-tuple-element.64.refs_2_), channel_id=1, source_target_pairs={{0,4},{4,8},{8,12},{12,14},{14,10},{10,6},{6,2},{2,0},{1,5},{5,9},... | collective-permute-start | bytes 688136 | tf_op jit(solution)/shard_map/ppermute | solution.py:207
  72.7 1.6 %collective-permute-start.27 = (bf16[32,3584]{1,0:T(8,128)(2,1)S(1)}, bf16[32,3584]{1,0:T(8,128)(2,1)S(1)}, u32[]{:S(2)}, u32[]{:S(2)}) collective-permute-start(bf16[32,3584]{1,0:T(8,128)(2,1)S(1)} %get-tuple-element.65.refs_2_), channel_id=1, source_target_pairs={{0,4},{4,8},{8,12},{12,14},{14,10},{10,6},{6,2},{2,0},{1,5},{5,9},... | collective-permute-start | bytes 688136 | tf_op jit(solution)/shard_map/ppermute | solution.py:207
  74.2 4.0 %collective-permute-done.21.refs_0_ = bf16[32,3584]{1,0:T(8,128)(2,1)S(1)} collective-permute-done((bf16[32,3584]{1,0:T(8,128)(2,1)S(1)}, bf16[32,3584]{1,0:T(8,128)(2,1)S(1)}, u32[]{:S(2)}, u32[]{:S(2)}) %collective-permute-start.21) | collective-permute-done | bytes 229408 | tf_op jit(solution)/shard_map/ppermute | solution.py:210
  79.4 1.6 %collective-permute-start.25 = (bf16[32,3584]{1,0:T(8,128)(2,1)S(1)}, bf16[32,3584]{1,0:T(8,128)(2,1)S(1)}, u32[]{:S(2)}, u32[]{:S(2)}) collective-permute-start(bf16[32,3584]{1,0:T(8,128)(2,1)S(1)} %get-tuple-element.67.refs_2_), channel_id=1, source_target_pairs={{0,4},{4,8},{8,12},{12,14},{14,10},{10,6},{6,2},{2,0},{1,5},{5,9},... | collective-permute-start | bytes 688136 | tf_op jit(solution)/shard_map/ppermute | solution.py:207
  80.9 2.2 %collective-permute-done.26.refs_0_ = bf16[32,3584]{1,0:T(8,128)(2,1)S(1)} collective-permute-done((bf16[32,3584]{1,0:T(8,128)(2,1)S(1)}, bf16[32,3584]{1,0:T(8,128)(2,1)S(1)}, u32[]{:S(2)}, u32[]{:S(2)}) %collective-permute-start.26) | collective-permute-done | bytes 229408 | tf_op jit(solution)/shard_map/ppermute | solution.py:210
  84.3 1.6 %collective-permute-start.31 = (bf16[32,3584]{1,0:T(8,128)(2,1)S(1)}, bf16[32,3584]{1,0:T(8,128)(2,1)S(1)}, u32[]{:S(2)}, u32[]{:S(2)}) collective-permute-start(bf16[32,3584]{1,0:T(8,128)(2,1)S(1)} %get-tuple-element.69.refs_2_), channel_id=1, source_target_pairs={{0,4},{4,8},{8,12},{12,14},{14,10},{10,6},{6,2},{2,0},{1,5},{5,9},... | collective-permute-start | bytes 688136 | tf_op jit(solution)/shard_map/ppermute | solution.py:207
  85.9 2.2 %collective-permute-done.24.refs_0_ = bf16[32,3584]{1,0:T(8,128)(2,1)S(1)} collective-permute-done((bf16[32,3584]{1,0:T(8,128)(2,1)S(1)}, bf16[32,3584]{1,0:T(8,128)(2,1)S(1)}, u32[]{:S(2)}, u32[]{:S(2)}) %collective-permute-start.24) | collective-permute-done | bytes 229408 | tf_op jit(solution)/shard_map/ppermute | solution.py:210
  88.7 1.6 %collective-permute-start.28 = (bf16[32,3584]{1,0:T(8,128)(2,1)S(1)}, bf16[32,3584]{1,0:T(8,128)(2,1)S(1)}, u32[]{:S(2)}, u32[]{:S(2)}) collective-permute-start(bf16[32,3584]{1,0:T(8,128)(2,1)S(1)} %get-tuple-element.70.refs_2_), channel_id=1, source_target_pairs={{0,4},{4,8},{8,12},{12,14},{14,10},{10,6},{6,2},{2,0},{1,5},{5,9},... | collective-permute-start | bytes 688136 | tf_op jit(solution)/shard_map/ppermute | solution.py:207
  93.6 1.6 %collective-permute-start.32 = (bf16[32,3584]{1,0:T(8,128)(2,1)S(1)}, bf16[32,3584]{1,0:T(8,128)(2,1)S(1)}, u32[]{:S(2)}, u32[]{:S(2)}) collective-permute-start(bf16[32,3584]{1,0:T(8,128)(2,1)S(1)} %get-tuple-element.73), channel_id=1, source_target_pairs={{0,4},{4,8},{8,12},{12,14},{14,10},{10,6},{6,2},{2,0},{1,5},{5,9},... | collective-permute-start | bytes 688136 | tf_op jit(solution)/shard_map/ppermute | solution.py:207
  95.7 2.7 %collective-permute-done.28.refs_0_ = bf16[32,3584]{1,0:T(8,128)(2,1)S(1)} collective-permute-done((bf16[32,3584]{1,0:T(8,128)(2,1)S(1)}, bf16[32,3584]{1,0:T(8,128)(2,1)S(1)}, u32[]{:S(2)}, u32[]{:S(2)}) %collective-permute-start.28) | collective-permute-done | bytes 229408 | tf_op jit(solution)/shard_map/ppermute | solution.py:207
  98.7 2.7 %collective-permute-done.32.refs_2_ = bf16[32,3584]{1,0:T(8,128)(2,1)S(1)} collective-permute-done((bf16[32,3584]{1,0:T(8,128)(2,1)S(1)}, bf16[32,3584]{1,0:T(8,128)(2,1)S(1)}, u32[]{:S(2)}, u32[]{:S(2)}) %collective-permute-start.32) | collective-permute-done | bytes 229408 | tf_op jit(solution)/shard_map/ppermute | solution.py:207
  (70 shorter events, 26.2 us)
Async XLA Ops:
  2.3 14.1 %collective-permute-start.2 = (bf16[64,3712]{1,0:T(8,128)(2,1)S(1)}, bf16[64,3712]{1,0:T(8,128)(2,1)S(1)}, u32[]{:S(2)}, u32[]{:S(2)}) collective-permute-start(bf16[64,3712]{1,0:T(8,128)(2,1)S(1)} %pack.1.refs_0_), channel_id=1, source_target_pairs={{0,4},{4,8},{8,12},{12,14},{14,10},{10,6},{6,2},{2,0},{1,5},{5,9},... | collective-permute-start | bytes 1425416 | tf_op jit(solution)/shard_map/ppermute | solution.py:207
  4.9 12.9 %collective-permute-start.3 = (bf16[64,3712]{1,0:T(8,128)(2,1)S(1)}, bf16[64,3712]{1,0:T(8,128)(2,1)S(1)}, u32[]{:S(2)}, u32[]{:S(2)}) collective-permute-start(bf16[64,3712]{1,0:T(8,128)(2,1)S(1)} %pack.1.refs_0_), channel_id=1, source_target_pairs={{4,0},{8,4},{12,8},{14,12},{10,14},{6,10},{2,6},{0,2},{5,1},{9,5},... | collective-permute-start | bytes 1425416 | tf_op jit(solution)/shard_map/ppermute | solution.py:210
  18.3 12.8 %collective-permute-start.7 = (bf16[64,3712]{1,0:T(8,128)(2,1)S(1)}, bf16[64,3712]{1,0:T(8,128)(2,1)S(1)}, u32[]{:S(2)}, u32[]{:S(2)}) collective-permute-start(bf16[64,3712]{1,0:T(8,128)(2,1)S(1)} %collective-permute-done.2.refs_0_), channel_id=1, source_target_pairs={{0,4},{4,8},{8,12},{12,14},{14,10},{10,6},{6,2},{2,0},{1,5},{5,9},... | collective-permute-start | bytes 1425416 | tf_op jit(solution)/shard_map/ppermute | solution.py:207
  19.9 12.5 %collective-permute-start.8 = (bf16[64,3712]{1,0:T(8,128)(2,1)S(1)}, bf16[64,3712]{1,0:T(8,128)(2,1)S(1)}, u32[]{:S(2)}, u32[]{:S(2)}) collective-permute-start(bf16[64,3712]{1,0:T(8,128)(2,1)S(1)} %collective-permute-done.3.refs_1_), channel_id=1, source_target_pairs={{4,0},{8,4},{12,8},{14,12},{10,14},{6,10},{2,6},{0,2},{5,1},{9,5},... | collective-permute-start | bytes 1425416 | tf_op jit(solution)/shard_map/ppermute | solution.py:210
  32.9 12.8 %collective-permute-start.12 = (bf16[64,3712]{1,0:T(8,128)(2,1)S(1)}, bf16[64,3712]{1,0:T(8,128)(2,1)S(1)}, u32[]{:S(2)}, u32[]{:S(2)}) collective-permute-start(bf16[64,3712]{1,0:T(8,128)(2,1)S(1)} %collective-permute-done.7.refs_0_), channel_id=1, source_target_pairs={{0,4},{4,8},{8,12},{12,14},{14,10},{10,6},{6,2},{2,0},{1,5},{5,9},... | collective-permute-start | bytes 1425416 | tf_op jit(solution)/shard_map/ppermute | solution.py:207
  34.5 12.5 %collective-permute-start.13 = (bf16[64,3712]{1,0:T(8,128)(2,1)S(1)}, bf16[64,3712]{1,0:T(8,128)(2,1)S(1)}, u32[]{:S(2)}, u32[]{:S(2)}) collective-permute-start(bf16[64,3712]{1,0:T(8,128)(2,1)S(1)} %collective-permute-done.8.refs_1_), channel_id=1, source_target_pairs={{4,0},{8,4},{12,8},{14,12},{10,14},{6,10},{2,6},{0,2},{5,1},{9,5},... | collective-permute-start | bytes 1425416 | tf_op jit(solution)/shard_map/ppermute | solution.py:210
  47.6 8.7 %collective-permute-start.17 = (bf16[64,3712]{1,0:T(8,128)(2,1)S(1)}, bf16[64,3712]{1,0:T(8,128)(2,1)S(1)}, u32[]{:S(2)}, u32[]{:S(2)}) collective-permute-start(bf16[64,3712]{1,0:T(8,128)(2,1)S(1)} %broadcast_select_fusion), channel_id=1, source_target_pairs={{0,4},{4,8},{8,12},{12,14},{14,10},{10,6},{6,2},{2,0},{5,1},{9,5},... | collective-permute-start | bytes 1425416 | tf_op jit(solution)/shard_map/ppermute | solution.py:259
  63.4 6.1 %collective-permute-start.20 = (bf16[32,3584]{1,0:T(8,128)(2,1)S(1)}, bf16[32,3584]{1,0:T(8,128)(2,1)S(1)}, u32[]{:S(2)}, u32[]{:S(2)}) collective-permute-start(bf16[32,3584]{1,0:T(8,128)(2,1)S(1)} %get-tuple-element.76), channel_id=1, source_target_pairs={{0,4},{4,8},{8,12},{12,14},{14,10},{10,6},{6,2},{2,0},{5,1},{9,5},... | collective-permute-start | bytes 688136 | tf_op jit(solution)/shard_map/ppermute | solution.py:265
  64.9 20.9 %collective-permute-start.6 = (bf16[128,3584]{1,0:T(8,128)(2,1)S(1)}, bf16[128,3584]{1,0:T(8,128)(2,1)S(1)}, u32[]{:S(2)}, u32[]{:S(2)}) collective-permute-start(bf16[128,3584]{1,0:T(8,128)(2,1)S(1)} %copy-done.1), channel_id=1, source_target_pairs={{0,1},{1,0},{2,3},{3,2},{4,5},{5,4},{6,7},{7,6},{8,9},{9,8},{10,11... | collective-permute-start | bytes 2752520 | tf_op jit(solution)/shard_map/ppermute | solution.py:213
  65.4 7.2 %collective-permute-start.11 = (bf16[128,3584]{1,0:T(8,128)(2,1)S(1)}, bf16[128,3584]{1,0:T(8,128)(2,1)S(1)}, u32[]{:S(2)}, u32[]{:S(2)}) collective-permute-start(bf16[128,3584]{1,0:T(8,128)(2,1)S(1)} %get-tuple-element.52), channel_id=1, source_target_pairs={{0,1},{1,0},{2,3},{3,2},{4,5},{5,4},{6,7},{7,6},{8,9},{9,8},{10,11... | collective-permute-start | bytes 2752520 | tf_op jit(solution)/shard_map/ppermute | solution.py:213
  65.4 6.5 %collective-permute-start.23 = (bf16[32,3584]{1,0:T(8,128)(2,1)S(1)}, bf16[32,3584]{1,0:T(8,128)(2,1)S(1)}, u32[]{:S(2)}, u32[]{:S(2)}) collective-permute-start(bf16[32,3584]{1,0:T(8,128)(2,1)S(1)} %get-tuple-element.75.refs_2_), channel_id=1, source_target_pairs={{0,4},{4,8},{8,12},{12,14},{14,10},{10,6},{6,2},{2,0},{5,1},{9,5},... | collective-permute-start | bytes 688136 | tf_op jit(solution)/shard_map/ppermute | solution.py:265
  69.7 8.6 %collective-permute-start.21 = (bf16[32,3584]{1,0:T(8,128)(2,1)S(1)}, bf16[32,3584]{1,0:T(8,128)(2,1)S(1)}, u32[]{:S(2)}, u32[]{:S(2)}) collective-permute-start(bf16[32,3584]{1,0:T(8,128)(2,1)S(1)} %get-tuple-element.63), channel_id=1, source_target_pairs={{4,0},{8,4},{12,8},{14,12},{10,14},{6,10},{2,6},{0,2},{5,1},{9,5},... | collective-permute-start | bytes 688136 | tf_op jit(solution)/shard_map/ppermute | solution.py:210
  70.2 8.5 %collective-permute-start.22 = (bf16[32,3584]{1,0:T(8,128)(2,1)S(1)}, bf16[32,3584]{1,0:T(8,128)(2,1)S(1)}, u32[]{:S(2)}, u32[]{:S(2)}) collective-permute-start(bf16[32,3584]{1,0:T(8,128)(2,1)S(1)} %get-tuple-element.64.refs_2_), channel_id=1, source_target_pairs={{0,4},{4,8},{8,12},{12,14},{14,10},{10,6},{6,2},{2,0},{1,5},{5,9},... | collective-permute-start | bytes 688136 | tf_op jit(solution)/shard_map/ppermute | solution.py:207
  72.2 11.0 %collective-permute-start.26 = (bf16[32,3584]{1,0:T(8,128)(2,1)S(1)}, bf16[32,3584]{1,0:T(8,128)(2,1)S(1)}, u32[]{:S(2)}, u32[]{:S(2)}) collective-permute-start(bf16[32,3584]{1,0:T(8,128)(2,1)S(1)} %get-tuple-element.68), channel_id=1, source_target_pairs={{4,0},{8,4},{12,8},{14,12},{10,14},{6,10},{2,6},{0,2},{5,1},{9,5},... | collective-permute-start | bytes 688136 | tf_op jit(solution)/shard_map/ppermute | solution.py:210
  72.7 10.9 %collective-permute-start.27 = (bf16[32,3584]{1,0:T(8,128)(2,1)S(1)}, bf16[32,3584]{1,0:T(8,128)(2,1)S(1)}, u32[]{:S(2)}, u32[]{:S(2)}) collective-permute-start(bf16[32,3584]{1,0:T(8,128)(2,1)S(1)} %get-tuple-element.65.refs_2_), channel_id=1, source_target_pairs={{0,4},{4,8},{8,12},{12,14},{14,10},{10,6},{6,2},{2,0},{1,5},{5,9},... | collective-permute-start | bytes 688136 | tf_op jit(solution)/shard_map/ppermute | solution.py:207
  78.9 9.2 %collective-permute-start.24 = (bf16[32,3584]{1,0:T(8,128)(2,1)S(1)}, bf16[32,3584]{1,0:T(8,128)(2,1)S(1)}, u32[]{:S(2)}, u32[]{:S(2)}) collective-permute-start(bf16[32,3584]{1,0:T(8,128)(2,1)S(1)} %get-tuple-element.66), channel_id=1, source_target_pairs={{4,0},{8,4},{12,8},{14,12},{10,14},{6,10},{2,6},{0,2},{5,1},{9,5},... | collective-permute-start | bytes 688136 | tf_op jit(solution)/shard_map/ppermute | solution.py:210
  79.4 9.2 %collective-permute-start.25 = (bf16[32,3584]{1,0:T(8,128)(2,1)S(1)}, bf16[32,3584]{1,0:T(8,128)(2,1)S(1)}, u32[]{:S(2)}, u32[]{:S(2)}) collective-permute-start(bf16[32,3584]{1,0:T(8,128)(2,1)S(1)} %get-tuple-element.67.refs_2_), channel_id=1, source_target_pairs={{0,4},{4,8},{8,12},{12,14},{14,10},{10,6},{6,2},{2,0},{1,5},{5,9},... | collective-permute-start | bytes 688136 | tf_op jit(solution)/shard_map/ppermute | solution.py:207
  83.8 8.1 %collective-permute-start.30 = (bf16[32,3584]{1,0:T(8,128)(2,1)S(1)}, bf16[32,3584]{1,0:T(8,128)(2,1)S(1)}, u32[]{:S(2)}, u32[]{:S(2)}) collective-permute-start(bf16[32,3584]{1,0:T(8,128)(2,1)S(1)} %get-tuple-element.72), channel_id=1, source_target_pairs={{4,0},{8,4},{12,8},{14,12},{10,14},{6,10},{2,6},{0,2},{5,1},{9,5},... | collective-permute-start | bytes 688136 | tf_op jit(solution)/shard_map/ppermute | solution.py:210
  84.3 9.2 %collective-permute-start.31 = (bf16[32,3584]{1,0:T(8,128)(2,1)S(1)}, bf16[32,3584]{1,0:T(8,128)(2,1)S(1)}, u32[]{:S(2)}, u32[]{:S(2)}) collective-permute-start(bf16[32,3584]{1,0:T(8,128)(2,1)S(1)} %get-tuple-element.69.refs_2_), channel_id=1, source_target_pairs={{0,4},{4,8},{8,12},{12,14},{14,10},{10,6},{6,2},{2,0},{1,5},{5,9},... | collective-permute-start | bytes 688136 | tf_op jit(solution)/shard_map/ppermute | solution.py:207
  85.9 9.8 %collective-permute-start.1 = (bf16[64,3584]{1,0:T(8,128)(2,1)S(1)}, bf16[64,3584]{1,0:T(8,128)(2,1)S(1)}, u32[]{:S(2)}, u32[]{:S(2)}) collective-permute-start(bf16[64,3584]{1,0:T(8,128)(2,1)S(1)} %copy-done.3), channel_id=1, source_target_pairs={{0,1},{1,0},{2,3},{3,2},{4,5},{5,4},{6,7},{7,6},{8,9},{9,8},{10,11... | collective-permute-start | bytes 1376264 | tf_op jit(solution)/shard_map/ppermute | solution.py:213
  88.7 9.7 %collective-permute-start.28 = (bf16[32,3584]{1,0:T(8,128)(2,1)S(1)}, bf16[32,3584]{1,0:T(8,128)(2,1)S(1)}, u32[]{:S(2)}, u32[]{:S(2)}) collective-permute-start(bf16[32,3584]{1,0:T(8,128)(2,1)S(1)} %get-tuple-element.70.refs_2_), channel_id=1, source_target_pairs={{0,4},{4,8},{8,12},{12,14},{14,10},{10,6},{6,2},{2,0},{1,5},{5,9},... | collective-permute-start | bytes 688136 | tf_op jit(solution)/shard_map/ppermute | solution.py:207
  90.3 8.3 %collective-permute-start.29 = (bf16[32,3584]{1,0:T(8,128)(2,1)S(1)}, bf16[32,3584]{1,0:T(8,128)(2,1)S(1)}, u32[]{:S(2)}, u32[]{:S(2)}) collective-permute-start(bf16[32,3584]{1,0:T(8,128)(2,1)S(1)} %get-tuple-element.71), channel_id=1, source_target_pairs={{4,0},{8,4},{12,8},{14,12},{10,14},{6,10},{2,6},{0,2},{5,1},{9,5},... | collective-permute-start | bytes 688136 | tf_op jit(solution)/shard_map/ppermute | solution.py:210
  93.6 7.8 %collective-permute-start.32 = (bf16[32,3584]{1,0:T(8,128)(2,1)S(1)}, bf16[32,3584]{1,0:T(8,128)(2,1)S(1)}, u32[]{:S(2)}, u32[]{:S(2)}) collective-permute-start(bf16[32,3584]{1,0:T(8,128)(2,1)S(1)} %get-tuple-element.73), channel_id=1, source_target_pairs={{0,4},{4,8},{8,12},{12,14},{14,10},{10,6},{6,2},{2,0},{1,5},{5,9},... | collective-permute-start | bytes 688136 | tf_op jit(solution)/shard_map/ppermute | solution.py:207
  95.2 6.1 %collective-permute-start.33 = (bf16[32,3584]{1,0:T(8,128)(2,1)S(1)}, bf16[32,3584]{1,0:T(8,128)(2,1)S(1)}, u32[]{:S(2)}, u32[]{:S(2)}) collective-permute-start(bf16[32,3584]{1,0:T(8,128)(2,1)S(1)} %get-tuple-element.74), channel_id=1, source_target_pairs={{4,0},{8,4},{12,8},{14,12},{10,14},{6,10},{2,6},{0,2},{5,1},{9,5},... | collective-permute-start | bytes 688136 | tf_op jit(solution)/shard_map/ppermute | solution.py:210
  (14 other events, 61.2 us)

commit v4 on v3

--- a/solution.py
+++ b/solution.py
@@ -22,8 +22,9 @@
         kept, (h_ref,) = sources, refs[6:]
     gate_ref, up_ref, down_ref = kept
     model_width, hidden_width = gate_ref.shape
-    hidden_cuts = [pl.ds(s, HIDDEN_TILE) for s in range(0, hidden_width, HIDDEN_TILE)]
-    out_cuts = [pl.ds(s, OUT_TILE) for s in range(0, model_width, OUT_TILE)]
+    hidden_tile, out_tile = (HIDDEN_TILE, OUT_TILE) if loads else (1024, 1792)
+    hidden_cuts = [pl.ds(s, hidden_tile) for s in range(0, hidden_width, hidden_tile)]
+    out_cuts = [pl.ds(s, out_tile) for s in range(0, model_width, out_tile)]
     order = [(which, cut) for cut in hidden_cuts for which in (0, 1)]
     order += [(2, cut) for cut in out_cuts]
     copies = []
@@ -72,7 +73,7 @@
     held = [pltpu.VMEM(w.shape, w.dtype) for w in weights]
     scratch = [pltpu.VMEM((rows, hidden_width), jnp.bfloat16)]
     out_shape = [result, result]
-    limit = 8
+    limit = 12
     if loads:
         steps = 2 * (hidden_width // HIDDEN_TILE) + model_width // OUT_TILE
         scratch.append(pltpu.SemaphoreType.DMA((steps,)))
@@ -123,10 +124,9 @@
     )(mine, other, *received, after)
 
 
-def pack_kernel(tokens_ref, routes_ref, gates_ref, out_ref, sem):
+def pack_kernel(tokens_ref, routes_ref, gates_ref, out_ref):
     model_width = tokens_ref.shape[1]
-    copy = pltpu.make_async_copy(tokens_ref, out_ref.at[:, pl.ds(0, model_width)], sem)
-    copy.start()
+    out_ref[:, :model_width] = tokens_ref[...]
     top_count, count = routes_ref.shape
     slot = lax.broadcasted_iota(jnp.int32, (LANES, count), 0)
     gates = gates_ref[...].astype(jnp.float32)
@@ -143,7 +143,6 @@
         preferred_element_type=jnp.float32,
     )
     out_ref[:, model_width:] = turned.astype(jnp.bfloat16)
-    copy.wait()
 
 
 def pack(tokens, routes, gate_values):
@@ -151,10 +150,9 @@
     count, model_width = tokens.shape
     return pl.pallas_call(
         pack_kernel,
-        in_specs=[pl.BlockSpec(memory_space=pl.ANY), vmem, vmem],
+        in_specs=[vmem, vmem, vmem],
         out_specs=vmem,
         out_shape=jax.ShapeDtypeStruct((count, model_width + LANES), jnp.bfloat16),
-        scratch_shapes=[pltpu.SemaphoreType.DMA],
         compiler_params=pltpu.CompilerParams(vmem_limit_bytes=4 * 1024 * 1024),
         name="pack",
     )(*[pltpu.with_memory_space_constraint(v, pltpu.HBM) for v in (tokens, routes.T, gate_values.T)])

time: 103 us -> 102 us (level)
  Pallas kernels: 37.4 us -> 36.1 us
  transfers between devices with their start and end apart: 34 -> 34, of which waited for: 23 -> 23; matrix products, arithmetic and copies ran while one was open for 0% -> 0% of each run, Pallas kernels for 31% -> 30%
where the time goes in v4:
time: 102 us
  waiting for transfers between devices  38.1 us (37%)
  Pallas kernels  36.1 us (35%)
  starting transfers between devices  25.6 us (25%)
  local copies, waits for them, and re-layouts  1.72 us (2%)
    pallas_call x5, Pallas kernels, expert(): pl.pallas_call(functools.partial(expert_kernel, count, loads), in_specs=[...  32.9 us
    ppermute x9, waiting for transfers between devices, onward(): return lax.ppermute(v, 'node', ring)  15.6 us
    ppermute x9, starting transfers between devices, onward(): return lax.ppermute(v, 'node', ring)  15.4 us
    ppermute x9, waiting for transfers between devices, backward(): return lax.ppermute(v, 'node', back)  14 us
    ppermute x9, starting transfers between devices, backward(): return lax.ppermute(v, 'node', back)  3.77 us
    ppermute x2, waiting for transfers between devices, shards(): got = [lax.ppermute(v, both, split) for v in sums]  3.77 us
    ppermute x13, waiting for transfers between devices, swap(): return lax.ppermute(v, 'local', [(0, 1), (1, 0)])  3.7 us
    ppermute x13, starting transfers between devices, swap(): return lax.ppermute(v, 'local', [(0, 1), (1, 0)])  2.7 us
  transfers between devices with their start and end apart: 34, of which 23 were waited for; matrix products, arithmetic and copies ran while one was open for 0% of the time, Pallas kernels for 30%

profile of v4, /device:TPU:0, one launch (start us, length us, event | category | flops | bytes accessed | tf_op | source)
XLA Modules:
  0.0 102.0 jit_solution(2246381829941430297)
XLA Ops:
  1.7 2.6 %collective-permute-start.2 = (bf16[64,3712]{1,0:T(8,128)(2,1)S(1)}, bf16[64,3712]{1,0:T(8,128)(2,1)S(1)}, u32[]{:S(2)}, u32[]{:S(2)}) collective-permute-start(bf16[64,3712]{1,0:T(8,128)(2,1)S(1)} %pack.1.refs_0_), channel_id=1, source_target_pairs={{0,4},{4,8},{8,12},{12,14},{14,10},{10,6},{6,2},{2,0},{1,5},{5,9},... | collective-permute-start | bytes 1425416 | tf_op jit(solution)/shard_map/ppermute | solution.py:205
  4.3 7.9 %expert.5 = (bf16[64,3584]{1,0:T(8,128)(2,1)S(1)}, bf16[64,3584]{1,0:T(8,128)(2,1)S(1)}, bf16[3584,1024]{1,0:T(8,128)(2,1)S(1)}, bf16[3584,1024]{1,0:T(8,128)(2,1)S(1)}, bf16[1024,3584]{1,0:T(8,128)(2,1)S(1)}) custom-call(bf16[64,3712]{1,0:T(8,128)(2,1)S(1)} %pack.1.refs_0_, bf16[64,3712]{1,0:T(8,128)(2,1)S(1)} %collective-permute-done.refs_1_, ...), custom_call_target="tpu_custom_call" | custom-call | flops 2818572288 | bytes 22020096 | tf_op jit(solution)/shard_map/expert/pallas_call | solution.py:87
  13.0 2.7 %collective-permute-done.2.refs_0_ = bf16[64,3712]{1,0:T(8,128)(2,1)S(1)} collective-permute-done((bf16[64,3712]{1,0:T(8,128)(2,1)S(1)}, bf16[64,3712]{1,0:T(8,128)(2,1)S(1)}, u32[]{:S(2)}, u32[]{:S(2)}) %collective-permute-start.2) | collective-permute-done | bytes 475168 | tf_op jit(solution)/shard_map/ppermute | solution.py:205
  17.8 1.6 %collective-permute-start.7 = (bf16[64,3712]{1,0:T(8,128)(2,1)S(1)}, bf16[64,3712]{1,0:T(8,128)(2,1)S(1)}, u32[]{:S(2)}, u32[]{:S(2)}) collective-permute-start(bf16[64,3712]{1,0:T(8,128)(2,1)S(1)} %collective-permute-done.2.refs_0_), channel_id=1, source_target_pairs={{0,4},{4,8},{8,12},{12,14},{14,10},{10,6},{6,2},{2,0},{1,5},{5,9},... | collective-permute-start | bytes 1425416 | tf_op jit(solution)/shard_map/ppermute | solution.py:205
  19.8 6.1 %expert.6 = (bf16[128,3584]{1,0:T(8,128)(2,1)S(1)}, bf16[128,3584]{1,0:T(8,128)(2,1)S(1)}) custom-call(bf16[64,3712]{1,0:T(8,128)(2,1)S(1)} %collective-permute-done.2.refs_0_, bf16[64,3712]{1,0:T(8,128)(2,1)S(1)} %collective-permute-done.3.refs_1_, bf16[64,3712]{1,0:T(8,128)(2,1)S(1)} %collective-permute-done.4.refs_2_, ...), custom_call_target="tpu_custom_call" | custom-call | flops 5637144576 | tf_op jit(solution)/shard_map/expert/pallas_call | solution.py:87
  26.9 3.7 %collective-permute-done.7.refs_0_ = bf16[64,3712]{1,0:T(8,128)(2,1)S(1)} collective-permute-done((bf16[64,3712]{1,0:T(8,128)(2,1)S(1)}, bf16[64,3712]{1,0:T(8,128)(2,1)S(1)}, u32[]{:S(2)}, u32[]{:S(2)}) %collective-permute-start.7) | collective-permute-done | bytes 475168 | tf_op jit(solution)/shard_map/ppermute | solution.py:205
  32.4 1.6 %collective-permute-start.12 = (bf16[64,3712]{1,0:T(8,128)(2,1)S(1)}, bf16[64,3712]{1,0:T(8,128)(2,1)S(1)}, u32[]{:S(2)}, u32[]{:S(2)}) collective-permute-start(bf16[64,3712]{1,0:T(8,128)(2,1)S(1)} %collective-permute-done.7.refs_0_), channel_id=1, source_target_pairs={{0,4},{4,8},{8,12},{12,14},{14,10},{10,6},{6,2},{2,0},{1,5},{5,9},... | collective-permute-start | bytes 1425416 | tf_op jit(solution)/shard_map/ppermute | solution.py:205
  34.4 9.8 %expert.7 = (bf16[128,3584]{1,0:T(8,128)(2,1)S(1)}, bf16[128,3584]{1,0:T(8,128)(2,1)S(1)}, bf16[3584,1024]{1,0:T(8,128)(2,1)S(1)}, bf16[3584,1024]{1,0:T(8,128)(2,1)S(1)}, bf16[1024,3584]{1,0:T(8,128)(2,1)S(1)}) custom-call(bf16[64,3712]{1,0:T(8,128)(2,1)S(1)} %collective-permute-done.7.refs_0_, bf16[64,3712]{1,0:T(8,128)(2,1)S(1)} %collective-permute-done.8.refs_1_, ...), custom_call_target="tpu_custom_call" | custom-call | flops 5637144576 | bytes 22020096 | tf_op jit(solution)/shard_map/expert/pallas_call | solution.py:87
  47.0 1.8 %collective-permute-start.17 = (bf16[64,3712]{1,0:T(8,128)(2,1)S(1)}, bf16[64,3712]{1,0:T(8,128)(2,1)S(1)}, u32[]{:S(2)}, u32[]{:S(2)}) collective-permute-start(bf16[64,3712]{1,0:T(8,128)(2,1)S(1)} %broadcast_select_fusion), channel_id=1, source_target_pairs={{0,4},{4,8},{8,12},{12,14},{14,10},{10,6},{6,2},{2,0},{5,1},{9,5},... | collective-permute-start | bytes 1425416 | tf_op jit(solution)/shard_map/ppermute | solution.py:257
  49.0 6.0 %expert.8 = (bf16[128,3584]{1,0:T(8,128)(2,1)S(1)}, bf16[128,3584]{1,0:T(8,128)(2,1)S(1)}) custom-call(bf16[64,3712]{1,0:T(8,128)(2,1)S(1)} %collective-permute-done.12.refs_0_, bf16[64,3712]{1,0:T(8,128)(2,1)S(1)} %collective-permute-done.13.refs_1_, bf16[64,3712]{1,0:T(8,128)(2,1)S(1)} %collective-permute-done.14.refs_2_, ...), custom_call_target="tpu_custom_call" | custom-call | flops 5637144576 | tf_op jit(solution)/shard_map/expert/pallas_call | solution.py:87
  55.9 1.8 %collective-permute-done.18.refs_1_ = bf16[64,3712]{1,0:T(8,128)(2,1)S(1)} collective-permute-done((bf16[64,3712]{1,0:T(8,128)(2,1)S(1)}, bf16[64,3712]{1,0:T(8,128)(2,1)S(1)}, u32[]{:S(2)}, u32[]{:S(2)}) %collective-permute-start.18) | collective-permute-done | bytes 475168 | tf_op jit(solution)/shard_map/ppermute | solution.py:211
  57.8 3.1 %expert.9 = (bf16[64,3584]{1,0:T(8,128)(2,1)S(1)}, bf16[64,3584]{1,0:T(8,128)(2,1)S(1)}) custom-call(bf16[64,3712]{1,0:T(8,128)(2,1)S(1)} %collective-permute-done.17.refs_0_, bf16[64,3712]{1,0:T(8,128)(2,1)S(1)} %collective-permute-done.18.refs_1_, f32[1,128]{1,0:T(1,128)S(1)} %compare_convert_fusion.refs_2_.refs_4_, ...), custom_call_target="tpu_custom_call" | custom-call | flops 2818572288 | tf_op jit(solution)/shard_map/expert/pallas_call | solution.py:87
  61.1 1.7 %collective-permute-done.19 = bf16[64,3584]{1,0:T(8,128)(2,1)S(1)} collective-permute-done((bf16[64,3584]{1,0:T(8,128)(2,1)S(1)}, bf16[64,3584]{1,0:T(8,128)(2,1)S(1)}, u32[]{:S(2)}, u32[]{:S(2)}) %collective-permute-start.19) | collective-permute-done | bytes 458784 | tf_op jit(solution)/shard_map/ppermute | solution.py:211
  65.5 3.5 %collective-permute-done.20 = bf16[32,3584]{1,0:T(8,128)(2,1)S(1)} collective-permute-done((bf16[32,3584]{1,0:T(8,128)(2,1)S(1)}, bf16[32,3584]{1,0:T(8,128)(2,1)S(1)}, u32[]{:S(2)}, u32[]{:S(2)}) %collective-permute-start.20) | collective-permute-done | bytes 229408 | tf_op jit(solution)/shard_map/ppermute | solution.py:263
  69.7 1.6 %collective-permute-start.22 = (bf16[32,3584]{1,0:T(8,128)(2,1)S(1)}, bf16[32,3584]{1,0:T(8,128)(2,1)S(1)}, u32[]{:S(2)}, u32[]{:S(2)}) collective-permute-start(bf16[32,3584]{1,0:T(8,128)(2,1)S(1)} %get-tuple-element.64.refs_2_), channel_id=1, source_target_pairs={{0,4},{4,8},{8,12},{12,14},{14,10},{10,6},{6,2},{2,0},{1,5},{5,9},... | collective-permute-start | bytes 688136 | tf_op jit(solution)/shard_map/ppermute | solution.py:205
  72.2 1.6 %collective-permute-start.27 = (bf16[32,3584]{1,0:T(8,128)(2,1)S(1)}, bf16[32,3584]{1,0:T(8,128)(2,1)S(1)}, u32[]{:S(2)}, u32[]{:S(2)}) collective-permute-start(bf16[32,3584]{1,0:T(8,128)(2,1)S(1)} %get-tuple-element.65.refs_2_), channel_id=1, source_target_pairs={{0,4},{4,8},{8,12},{12,14},{14,10},{10,6},{6,2},{2,0},{1,5},{5,9},... | collective-permute-start | bytes 688136 | tf_op jit(solution)/shard_map/ppermute | solution.py:205
  73.8 4.0 %collective-permute-done.21.refs_0_ = bf16[32,3584]{1,0:T(8,128)(2,1)S(1)} collective-permute-done((bf16[32,3584]{1,0:T(8,128)(2,1)S(1)}, bf16[32,3584]{1,0:T(8,128)(2,1)S(1)}, u32[]{:S(2)}, u32[]{:S(2)}) %collective-permute-start.21) | collective-permute-done | bytes 229408 | tf_op jit(solution)/shard_map/ppermute | solution.py:208
  78.9 1.6 %collective-permute-start.25 = (bf16[32,3584]{1,0:T(8,128)(2,1)S(1)}, bf16[32,3584]{1,0:T(8,128)(2,1)S(1)}, u32[]{:S(2)}, u32[]{:S(2)}) collective-permute-start(bf16[32,3584]{1,0:T(8,128)(2,1)S(1)} %get-tuple-element.67.refs_2_), channel_id=1, source_target_pairs={{0,4},{4,8},{8,12},{12,14},{14,10},{10,6},{6,2},{2,0},{1,5},{5,9},... | collective-permute-start | bytes 688136 | tf_op jit(solution)/shard_map/ppermute | solution.py:205
  80.5 2.2 %collective-permute-done.26.refs_0_ = bf16[32,3584]{1,0:T(8,128)(2,1)S(1)} collective-permute-done((bf16[32,3584]{1,0:T(8,128)(2,1)S(1)}, bf16[32,3584]{1,0:T(8,128)(2,1)S(1)}, u32[]{:S(2)}, u32[]{:S(2)}) %collective-permute-start.26) | collective-permute-done | bytes 229408 | tf_op jit(solution)/shard_map/ppermute | solution.py:208
  85.4 2.2 %collective-permute-done.24.refs_0_ = bf16[32,3584]{1,0:T(8,128)(2,1)S(1)} collective-permute-done((bf16[32,3584]{1,0:T(8,128)(2,1)S(1)}, bf16[32,3584]{1,0:T(8,128)(2,1)S(1)}, u32[]{:S(2)}, u32[]{:S(2)}) %collective-permute-start.24) | collective-permute-done | bytes 229408 | tf_op jit(solution)/shard_map/ppermute | solution.py:208
  88.3 1.6 %collective-permute-start.28 = (bf16[32,3584]{1,0:T(8,128)(2,1)S(1)}, bf16[32,3584]{1,0:T(8,128)(2,1)S(1)}, u32[]{:S(2)}, u32[]{:S(2)}) collective-permute-start(bf16[32,3584]{1,0:T(8,128)(2,1)S(1)} %get-tuple-element.70.refs_2_), channel_id=1, source_target_pairs={{0,4},{4,8},{8,12},{12,14},{14,10},{10,6},{6,2},{2,0},{1,5},{5,9},... | collective-permute-start | bytes 688136 | tf_op jit(solution)/shard_map/ppermute | solution.py:205
  93.2 1.6 %collective-permute-start.32 = (bf16[32,3584]{1,0:T(8,128)(2,1)S(1)}, bf16[32,3584]{1,0:T(8,128)(2,1)S(1)}, u32[]{:S(2)}, u32[]{:S(2)}) collective-permute-start(bf16[32,3584]{1,0:T(8,128)(2,1)S(1)} %get-tuple-element.73), channel_id=1, source_target_pairs={{0,4},{4,8},{8,12},{12,14},{14,10},{10,6},{6,2},{2,0},{1,5},{5,9},... | collective-permute-start | bytes 688136 | tf_op jit(solution)/shard_map/ppermute | solution.py:205
  95.3 2.7 %collective-permute-done.28.refs_0_ = bf16[32,3584]{1,0:T(8,128)(2,1)S(1)} collective-permute-done((bf16[32,3584]{1,0:T(8,128)(2,1)S(1)}, bf16[32,3584]{1,0:T(8,128)(2,1)S(1)}, u32[]{:S(2)}, u32[]{:S(2)}) %collective-permute-start.28) | collective-permute-done | bytes 229408 | tf_op jit(solution)/shard_map/ppermute | solution.py:205
  98.2 2.7 %collective-permute-done.32.refs_2_ = bf16[32,3584]{1,0:T(8,128)(2,1)S(1)} collective-permute-done((bf16[32,3584]{1,0:T(8,128)(2,1)S(1)}, bf16[32,3584]{1,0:T(8,128)(2,1)S(1)}, u32[]{:S(2)}, u32[]{:S(2)}) %collective-permute-start.32) | collective-permute-done | bytes 229408 | tf_op jit(solution)/shard_map/ppermute | solution.py:205
  (70 shorter events, 26.0 us)
Async XLA Ops:
  1.7 14.1 %collective-permute-start.2 = (bf16[64,3712]{1,0:T(8,128)(2,1)S(1)}, bf16[64,3712]{1,0:T(8,128)(2,1)S(1)}, u32[]{:S(2)}, u32[]{:S(2)}) collective-permute-start(bf16[64,3712]{1,0:T(8,128)(2,1)S(1)} %pack.1.refs_0_), channel_id=1, source_target_pairs={{0,4},{4,8},{8,12},{12,14},{14,10},{10,6},{6,2},{2,0},{1,5},{5,9},... | collective-permute-start | bytes 1425416 | tf_op jit(solution)/shard_map/ppermute | solution.py:205
  4.3 13.0 %collective-permute-start.3 = (bf16[64,3712]{1,0:T(8,128)(2,1)S(1)}, bf16[64,3712]{1,0:T(8,128)(2,1)S(1)}, u32[]{:S(2)}, u32[]{:S(2)}) collective-permute-start(bf16[64,3712]{1,0:T(8,128)(2,1)S(1)} %pack.1.refs_0_), channel_id=1, source_target_pairs={{4,0},{8,4},{12,8},{14,12},{10,14},{6,10},{2,6},{0,2},{5,1},{9,5},... | collective-permute-start | bytes 1425416 | tf_op jit(solution)/shard_map/ppermute | solution.py:208
  17.8 12.8 %collective-permute-start.7 = (bf16[64,3712]{1,0:T(8,128)(2,1)S(1)}, bf16[64,3712]{1,0:T(8,128)(2,1)S(1)}, u32[]{:S(2)}, u32[]{:S(2)}) collective-permute-start(bf16[64,3712]{1,0:T(8,128)(2,1)S(1)} %collective-permute-done.2.refs_0_), channel_id=1, source_target_pairs={{0,4},{4,8},{8,12},{12,14},{14,10},{10,6},{6,2},{2,0},{1,5},{5,9},... | collective-permute-start | bytes 1425416 | tf_op jit(solution)/shard_map/ppermute | solution.py:205
  19.4 12.5 %collective-permute-start.8 = (bf16[64,3712]{1,0:T(8,128)(2,1)S(1)}, bf16[64,3712]{1,0:T(8,128)(2,1)S(1)}, u32[]{:S(2)}, u32[]{:S(2)}) collective-permute-start(bf16[64,3712]{1,0:T(8,128)(2,1)S(1)} %collective-permute-done.3.refs_1_), channel_id=1, source_target_pairs={{4,0},{8,4},{12,8},{14,12},{10,14},{6,10},{2,6},{0,2},{5,1},{9,5},... | collective-permute-start | bytes 1425416 | tf_op jit(solution)/shard_map/ppermute | solution.py:208
  32.4 12.8 %collective-permute-start.12 = (bf16[64,3712]{1,0:T(8,128)(2,1)S(1)}, bf16[64,3712]{1,0:T(8,128)(2,1)S(1)}, u32[]{:S(2)}, u32[]{:S(2)}) collective-permute-start(bf16[64,3712]{1,0:T(8,128)(2,1)S(1)} %collective-permute-done.7.refs_0_), channel_id=1, source_target_pairs={{0,4},{4,8},{8,12},{12,14},{14,10},{10,6},{6,2},{2,0},{1,5},{5,9},... | collective-permute-start | bytes 1425416 | tf_op jit(solution)/shard_map/ppermute | solution.py:205
  33.9 12.5 %collective-permute-start.13 = (bf16[64,3712]{1,0:T(8,128)(2,1)S(1)}, bf16[64,3712]{1,0:T(8,128)(2,1)S(1)}, u32[]{:S(2)}, u32[]{:S(2)}) collective-permute-start(bf16[64,3712]{1,0:T(8,128)(2,1)S(1)} %collective-permute-done.8.refs_1_), channel_id=1, source_target_pairs={{4,0},{8,4},{12,8},{14,12},{10,14},{6,10},{2,6},{0,2},{5,1},{9,5},... | collective-permute-start | bytes 1425416 | tf_op jit(solution)/shard_map/ppermute | solution.py:208
  47.0 8.9 %collective-permute-start.17 = (bf16[64,3712]{1,0:T(8,128)(2,1)S(1)}, bf16[64,3712]{1,0:T(8,128)(2,1)S(1)}, u32[]{:S(2)}, u32[]{:S(2)}) collective-permute-start(bf16[64,3712]{1,0:T(8,128)(2,1)S(1)} %broadcast_select_fusion), channel_id=1, source_target_pairs={{0,4},{4,8},{8,12},{12,14},{14,10},{10,6},{6,2},{2,0},{5,1},{9,5},... | collective-permute-start | bytes 1425416 | tf_op jit(solution)/shard_map/ppermute | solution.py:257
  62.9 6.1 %collective-permute-start.20 = (bf16[32,3584]{1,0:T(8,128)(2,1)S(1)}, bf16[32,3584]{1,0:T(8,128)(2,1)S(1)}, u32[]{:S(2)}, u32[]{:S(2)}) collective-permute-start(bf16[32,3584]{1,0:T(8,128)(2,1)S(1)} %get-tuple-element.76), channel_id=1, source_target_pairs={{0,4},{4,8},{8,12},{12,14},{14,10},{10,6},{6,2},{2,0},{5,1},{9,5},... | collective-permute-start | bytes 688136 | tf_op jit(solution)/shard_map/ppermute | solution.py:263
  64.5 20.9 %collective-permute-start.6 = (bf16[128,3584]{1,0:T(8,128)(2,1)S(1)}, bf16[128,3584]{1,0:T(8,128)(2,1)S(1)}, u32[]{:S(2)}, u32[]{:S(2)}) collective-permute-start(bf16[128,3584]{1,0:T(8,128)(2,1)S(1)} %copy-done.1), channel_id=1, source_target_pairs={{0,1},{1,0},{2,3},{3,2},{4,5},{5,4},{6,7},{7,6},{8,9},{9,8},{10,11... | collective-permute-start | bytes 2752520 | tf_op jit(solution)/shard_map/ppermute | solution.py:211
  65.0 7.2 %collective-permute-start.11 = (bf16[128,3584]{1,0:T(8,128)(2,1)S(1)}, bf16[128,3584]{1,0:T(8,128)(2,1)S(1)}, u32[]{:S(2)}, u32[]{:S(2)}) collective-permute-start(bf16[128,3584]{1,0:T(8,128)(2,1)S(1)} %get-tuple-element.52), channel_id=1, source_target_pairs={{0,1},{1,0},{2,3},{3,2},{4,5},{5,4},{6,7},{7,6},{8,9},{9,8},{10,11... | collective-permute-start | bytes 2752520 | tf_op jit(solution)/shard_map/ppermute | solution.py:211
  65.0 6.5 %collective-permute-start.23 = (bf16[32,3584]{1,0:T(8,128)(2,1)S(1)}, bf16[32,3584]{1,0:T(8,128)(2,1)S(1)}, u32[]{:S(2)}, u32[]{:S(2)}) collective-permute-start(bf16[32,3584]{1,0:T(8,128)(2,1)S(1)} %get-tuple-element.75.refs_2_), channel_id=1, source_target_pairs={{0,4},{4,8},{8,12},{12,14},{14,10},{10,6},{6,2},{2,0},{5,1},{9,5},... | collective-permute-start | bytes 688136 | tf_op jit(solution)/shard_map/ppermute | solution.py:263
  69.2 8.6 %collective-permute-start.21 = (bf16[32,3584]{1,0:T(8,128)(2,1)S(1)}, bf16[32,3584]{1,0:T(8,128)(2,1)S(1)}, u32[]{:S(2)}, u32[]{:S(2)}) collective-permute-start(bf16[32,3584]{1,0:T(8,128)(2,1)S(1)} %get-tuple-element.63), channel_id=1, source_target_pairs={{4,0},{8,4},{12,8},{14,12},{10,14},{6,10},{2,6},{0,2},{5,1},{9,5},... | collective-permute-start | bytes 688136 | tf_op jit(solution)/shard_map/ppermute | solution.py:208
  69.7 8.5 %collective-permute-start.22 = (bf16[32,3584]{1,0:T(8,128)(2,1)S(1)}, bf16[32,3584]{1,0:T(8,128)(2,1)S(1)}, u32[]{:S(2)}, u32[]{:S(2)}) collective-permute-start(bf16[32,3584]{1,0:T(8,128)(2,1)S(1)} %get-tuple-element.64.refs_2_), channel_id=1, source_target_pairs={{0,4},{4,8},{8,12},{12,14},{14,10},{10,6},{6,2},{2,0},{1,5},{5,9},... | collective-permute-start | bytes 688136 | tf_op jit(solution)/shard_map/ppermute | solution.py:205
  71.8 11.0 %collective-permute-start.26 = (bf16[32,3584]{1,0:T(8,128)(2,1)S(1)}, bf16[32,3584]{1,0:T(8,128)(2,1)S(1)}, u32[]{:S(2)}, u32[]{:S(2)}) collective-permute-start(bf16[32,3584]{1,0:T(8,128)(2,1)S(1)} %get-tuple-element.68), channel_id=1, source_target_pairs={{4,0},{8,4},{12,8},{14,12},{10,14},{6,10},{2,6},{0,2},{5,1},{9,5},... | collective-permute-start | bytes 688136 | tf_op jit(solution)/shard_map/ppermute | solution.py:208
  72.2 11.0 %collective-permute-start.27 = (bf16[32,3584]{1,0:T(8,128)(2,1)S(1)}, bf16[32,3584]{1,0:T(8,128)(2,1)S(1)}, u32[]{:S(2)}, u32[]{:S(2)}) collective-permute-start(bf16[32,3584]{1,0:T(8,128)(2,1)S(1)} %get-tuple-element.65.refs_2_), channel_id=1, source_target_pairs={{0,4},{4,8},{8,12},{12,14},{14,10},{10,6},{6,2},{2,0},{1,5},{5,9},... | collective-permute-start | bytes 688136 | tf_op jit(solution)/shard_map/ppermute | solution.py:205
  78.4 9.2 %collective-permute-start.24 = (bf16[32,3584]{1,0:T(8,128)(2,1)S(1)}, bf16[32,3584]{1,0:T(8,128)(2,1)S(1)}, u32[]{:S(2)}, u32[]{:S(2)}) collective-permute-start(bf16[32,3584]{1,0:T(8,128)(2,1)S(1)} %get-tuple-element.66), channel_id=1, source_target_pairs={{4,0},{8,4},{12,8},{14,12},{10,14},{6,10},{2,6},{0,2},{5,1},{9,5},... | collective-permute-start | bytes 688136 | tf_op jit(solution)/shard_map/ppermute | solution.py:208
  78.9 9.2 %collective-permute-start.25 = (bf16[32,3584]{1,0:T(8,128)(2,1)S(1)}, bf16[32,3584]{1,0:T(8,128)(2,1)S(1)}, u32[]{:S(2)}, u32[]{:S(2)}) collective-permute-start(bf16[32,3584]{1,0:T(8,128)(2,1)S(1)} %get-tuple-element.67.refs_2_), channel_id=1, source_target_pairs={{0,4},{4,8},{8,12},{12,14},{14,10},{10,6},{6,2},{2,0},{1,5},{5,9},... | collective-permute-start | bytes 688136 | tf_op jit(solution)/shard_map/ppermute | solution.py:205
  83.4 8.1 %collective-permute-start.30 = (bf16[32,3584]{1,0:T(8,128)(2,1)S(1)}, bf16[32,3584]{1,0:T(8,128)(2,1)S(1)}, u32[]{:S(2)}, u32[]{:S(2)}) collective-permute-start(bf16[32,3584]{1,0:T(8,128)(2,1)S(1)} %get-tuple-element.72), channel_id=1, source_target_pairs={{4,0},{8,4},{12,8},{14,12},{10,14},{6,10},{2,6},{0,2},{5,1},{9,5},... | collective-permute-start | bytes 688136 | tf_op jit(solution)/shard_map/ppermute | solution.py:208
  83.9 9.2 %collective-permute-start.31 = (bf16[32,3584]{1,0:T(8,128)(2,1)S(1)}, bf16[32,3584]{1,0:T(8,128)(2,1)S(1)}, u32[]{:S(2)}, u32[]{:S(2)}) collective-permute-start(bf16[32,3584]{1,0:T(8,128)(2,1)S(1)} %get-tuple-element.69.refs_2_), channel_id=1, source_target_pairs={{0,4},{4,8},{8,12},{12,14},{14,10},{10,6},{6,2},{2,0},{1,5},{5,9},... | collective-permute-start | bytes 688136 | tf_op jit(solution)/shard_map/ppermute | solution.py:205
  85.4 9.8 %collective-permute-start.1 = (bf16[64,3584]{1,0:T(8,128)(2,1)S(1)}, bf16[64,3584]{1,0:T(8,128)(2,1)S(1)}, u32[]{:S(2)}, u32[]{:S(2)}) collective-permute-start(bf16[64,3584]{1,0:T(8,128)(2,1)S(1)} %copy-done.3), channel_id=1, source_target_pairs={{0,1},{1,0},{2,3},{3,2},{4,5},{5,4},{6,7},{7,6},{8,9},{9,8},{10,11... | collective-permute-start | bytes 1376264 | tf_op jit(solution)/shard_map/ppermute | solution.py:211
  88.3 9.7 %collective-permute-start.28 = (bf16[32,3584]{1,0:T(8,128)(2,1)S(1)}, bf16[32,3584]{1,0:T(8,128)(2,1)S(1)}, u32[]{:S(2)}, u32[]{:S(2)}) collective-permute-start(bf16[32,3584]{1,0:T(8,128)(2,1)S(1)} %get-tuple-element.70.refs_2_), channel_id=1, source_target_pairs={{0,4},{4,8},{8,12},{12,14},{14,10},{10,6},{6,2},{2,0},{1,5},{5,9},... | collective-permute-start | bytes 688136 | tf_op jit(solution)/shard_map/ppermute | solution.py:205
  89.9 8.3 %collective-permute-start.29 = (bf16[32,3584]{1,0:T(8,128)(2,1)S(1)}, bf16[32,3584]{1,0:T(8,128)(2,1)S(1)}, u32[]{:S(2)}, u32[]{:S(2)}) collective-permute-start(bf16[32,3584]{1,0:T(8,128)(2,1)S(1)} %get-tuple-element.71), channel_id=1, source_target_pairs={{4,0},{8,4},{12,8},{14,12},{10,14},{6,10},{2,6},{0,2},{5,1},{9,5},... | collective-permute-start | bytes 688136 | tf_op jit(solution)/shard_map/ppermute | solution.py:208
  93.2 7.8 %collective-permute-start.32 = (bf16[32,3584]{1,0:T(8,128)(2,1)S(1)}, bf16[32,3584]{1,0:T(8,128)(2,1)S(1)}, u32[]{:S(2)}, u32[]{:S(2)}) collective-permute-start(bf16[32,3584]{1,0:T(8,128)(2,1)S(1)} %get-tuple-element.73), channel_id=1, source_target_pairs={{0,4},{4,8},{8,12},{12,14},{14,10},{10,6},{6,2},{2,0},{1,5},{5,9},... | collective-permute-start | bytes 688136 | tf_op jit(solution)/shard_map/ppermute | solution.py:205
  94.8 6.1 %collective-permute-start.33 = (bf16[32,3584]{1,0:T(8,128)(2,1)S(1)}, bf16[32,3584]{1,0:T(8,128)(2,1)S(1)}, u32[]{:S(2)}, u32[]{:S(2)}) collective-permute-start(bf16[32,3584]{1,0:T(8,128)(2,1)S(1)} %get-tuple-element.74), channel_id=1, source_target_pairs={{4,0},{8,4},{12,8},{14,12},{10,14},{6,10},{2,6},{0,2},{5,1},{9,5},... | collective-permute-start | bytes 688136 | tf_op jit(solution)/shard_map/ppermute | solution.py:208
  (14 other events, 61.2 us)
